TPU v7x, 32 devices: a whole 2x2x4 slice. The times are simulated.
32 devices in a mesh: lon: 8 (over z, core), lat: 2 (over y), tp: 2 (over x).
Axes of the slice: x: 2, y: 2, z: 4, core: 2. Of those that a mesh axis runs over, the one named last changes fastest.
Arguments:
- latent: bfloat16 [96, 24, 4, 512], P('lon', 'lat'), may hold values from -6 to 6
- cotangent: bfloat16 [96, 24, 4, 512], P('lon', 'lat'), may hold values from -6 to 6
- ln_gain: float32 [512], replicated, may hold values from 0.1 to 1.9
- w_qkv: bfloat16 [3, 512, 512], P(None, None, 'tp'), may hold values from -0.25 to 0.25
- w_out: bfloat16 [512, 512], P('tp'), may hold values from -0.25 to 0.25
- bias_table: float32 [4, 2, 8, 3312], P('lat', None, 'tp'), may hold values from -3 to 360
Outputs:
- output: bfloat16 [96, 24, 4, 512], P('lon', 'lat')
- grad_latent: bfloat16 [96, 24, 4, 512], P('lon', 'lat')
- grad_gain: float32 [512], replicated
- grad_wqkv: float32 [3, 512, 512], P(None, None, 'tp')
- grad_wout: float32 [512, 512], P('tp')
- grad_bias: float32 [4, 2, 8, 3312], P('lat', None, 'tp')
All inputs are finite; a program needn't handle non-finite values.
Results may differ from a plain program's by a relative error of at most 0.023.
Values may be sent and summed in bfloat16 or wider, within the bound.
A program may use at most 128 MiB of HBM per device.

v0:
```python
import math

import jax
import jax.numpy as jnp
import numpy as np
from jax import lax
from jax.sharding import PartitionSpec as P

HD = 64
WLON = 12
WLAT = 6
WLEV = 2
WTOK = 144
NREL = 3312


def passed_along(shard, axis, by):
    count = lax.axis_size(axis)
    return lax.ppermute(shard, axis, [(i, (i + by) % count) for i in range(count)])


def pair_layout():
    position = np.arange(WTOK)
    lon_pos = position // (WLAT * WLEV)
    lat_pos = position // WLEV % WLAT
    lev_pos = position % WLEV
    relative = lon_pos[None, :] - lon_pos[:, None] + WLON - 1
    entries = (
        (lev_pos[:, None] * WLEV + lev_pos[None, :]) * WLAT * WLAT
        + lat_pos[:, None] * WLAT
        + lat_pos[None, :]
    ) * (2 * WLON - 1) + relative
    return (entries.astype(np.int32), lat_pos, lev_pos)


def to_windows(values):
    lon_cells, lat_cells, lev_cells, channels = values.shape
    blocks = values.reshape(
        lon_cells // WLON, WLON, lat_cells // WLAT, WLAT, lev_cells // WLEV, WLEV, channels
    )
    blocks = blocks.transpose(2, 4, 0, 1, 3, 5, 6)
    return blocks.reshape(lat_cells // WLAT, lev_cells // WLEV, lon_cells // WLON, WTOK, channels)


def from_windows(values):
    lat_bands, lev_bands, lon_bands, window_len, channels = values.shape
    blocks = values.reshape(lat_bands, lev_bands, lon_bands, WLON, WLAT, WLEV, channels)
    blocks = blocks.transpose(2, 3, 0, 4, 1, 5, 6)
    return blocks.reshape(lon_bands * WLON, lat_bands * WLAT, lev_bands * WLEV, channels)


def allowed_pairs(last_lat, lev_bands, lat_pos, lev_pos):
    lat_edge = jnp.asarray(lat_pos >= WLAT - WLAT // 2)
    lev_edge = jnp.asarray(lev_pos >= WLEV - WLEV // 2)
    lev_last = jnp.arange(lev_bands) == lev_bands - 1
    lat_region = last_lat[:, None] & lat_edge[None, :]
    lev_region = lev_last[:, None] & lev_edge[None, :]
    same_lat = lat_region[:, :, None] == lat_region[:, None, :]
    same_lev = lev_region[:, :, None] == lev_region[:, None, :]
    return same_lat[:, None] & same_lev[None, :]


def layer_norm(values, scale_gain):
    values = values.astype(jnp.float32)
    centre = jnp.mean(values, -1, keepdims=True)
    shifted = values - centre
    inv_std = lax.rsqrt(jnp.mean(shifted * shifted, -1, keepdims=True) + 1e-05)
    normed = shifted * inv_std
    return (normed, inv_std, (normed * scale_gain).astype(jnp.bfloat16))


def enter(values, lon_move, lat_move):
    lon_half = WLON // 2
    lat_half = WLAT // 2
    arrived = lon_move(values[:lon_half])
    values = jnp.concatenate([values[lon_half:], arrived], 0)
    arrived = lat_move(values[:, :lat_half])
    values = jnp.concatenate([values[:, lat_half:], arrived], 1)
    return jnp.roll(values, -(WLEV // 2), axis=2)


def leave(values, lon_move, lat_move):
    lon_half = WLON // 2
    lat_half = WLAT // 2
    values = jnp.roll(values, WLEV // 2, axis=2)
    arrived = lat_move(values[:, values.shape[1] - lat_half :])
    values = jnp.concatenate([arrived, values[:, : values.shape[1] - lat_half]], 1)
    arrived = lon_move(values[values.shape[0] - lon_half :])
    values = jnp.concatenate([arrived, values[: values.shape[0] - lon_half]], 0)
    return values


def head_total(partial_value):
    return lax.psum(partial_value.astype(jnp.bfloat16), "tp").astype(jnp.float32)


def on_device(latent, cotangent, ln_gain, w_qkv, w_out, bias_table):
    lon_cells, lat_cells, lev_cells, model_width = latent.shape
    local_width = w_out.shape[0]
    head_count = local_width // HD
    lat_bands = lat_cells // WLAT
    lev_bands = lev_cells // WLEV
    lon_bands = lon_cells // WLON
    entries, lat_pos, lev_pos = pair_layout()
    entry_ids = jnp.asarray(entries)
    inv_scale = 1.0 / math.sqrt(HD)
    last_device = lax.axis_index("lat") == lax.axis_size("lat") - 1
    last_lat = last_device & (jnp.arange(lat_bands) == lat_bands - 1)
    allowed = allowed_pairs(last_lat, lev_bands, lat_pos, lev_pos)
    bias_full = jnp.take(bias_table, entry_ids, axis=3)
    head_shape = (lat_bands, lev_bands, lon_bands, WTOK, head_count, HD)
    win_shape = (lat_bands, lev_bands, lon_bands, WTOK, model_width)
    joined = jnp.concatenate([latent, cotangent], 3)
    rolled = enter(
        joined,
        lambda border: passed_along(border, "lon", -1),
        lambda border: passed_along(border, "lat", -1),
    )
    windows = to_windows(rolled)
    latent_win = windows[..., :model_width]
    upstream = windows[..., model_width:]
    hidden = layer_norm(latent_win, ln_gain)[2]
    hidden_flat = hidden.reshape(-1, model_width)
    projected = [
        jnp.dot(hidden_flat, w_qkv[member], preferred_element_type=jnp.float32).astype(jnp.bfloat16)
        for member in range(3)
    ]
    queries, key_rows, value_rows = [matrix.reshape(head_shape) for matrix in projected]
    scores = (
        jnp.einsum("abwqhe,abwkhe->abwhqk", queries, key_rows, preferred_element_type=jnp.float32)
        * inv_scale
        + bias_full[:, :, None]
    )
    scores = jnp.where(allowed[:, :, None, None], scores, -jnp.inf)
    row_max = jnp.max(scores, -1, keepdims=True)
    expsum = jnp.exp(scores - row_max)
    attn_weights = expsum / jnp.sum(expsum, -1, keepdims=True)
    attn_low = attn_weights.astype(jnp.bfloat16)
    attended = jnp.einsum(
        "abwhqk,abwkhe->abwqhe", attn_low, value_rows, preferred_element_type=jnp.float32
    ).astype(jnp.bfloat16)
    attended_flat = attended.reshape(-1, local_width)
    out_win = head_total(jnp.dot(attended_flat, w_out, preferred_element_type=jnp.float32)).astype(
        jnp.bfloat16
    )
    out_own = leave(
        from_windows(out_win.reshape(win_shape)),
        lambda border: passed_along(border, "lon", 1),
        lambda border: passed_along(border, "lat", 1),
    )
    cot_flat = upstream.reshape(-1, model_width)
    grad_out_local = jnp.dot(attended_flat.T, cot_flat, preferred_element_type=jnp.float32)
    down_heads = (
        jnp.dot(cot_flat, w_out.T, preferred_element_type=jnp.float32)
        .astype(jnp.bfloat16)
        .reshape(head_shape)
    )
    output = (latent.astype(jnp.float32) + out_own.astype(jnp.float32)).astype(jnp.bfloat16)
    down_scores = jnp.einsum(
        "abwqhe,abwkhe->abwhqk", down_heads, value_rows, preferred_element_type=jnp.float32
    )
    grad_values = jnp.einsum(
        "abwhqk,abwqhe->abwkhe", attn_low, down_heads, preferred_element_type=jnp.float32
    ).astype(jnp.bfloat16)
    centred = jnp.sum(down_scores * attn_weights, -1, keepdims=True)
    grad_scores = attn_weights * (down_scores - centred)
    bias_terms = jnp.sum(grad_scores, 2)
    grad_bias_local = jax.ops.segment_sum(
        bias_terms.reshape(-1, WTOK * WTOK).T, entry_ids.reshape(-1), num_segments=NREL
    ).T
    grad_bias_local = grad_bias_local.reshape(bias_table.shape)
    scores_low = grad_scores.astype(jnp.bfloat16)
    grad_queries = (
        jnp.einsum(
            "abwhqk,abwkhe->abwqhe", scores_low, key_rows, preferred_element_type=jnp.float32
        )
        * inv_scale
    ).astype(jnp.bfloat16)
    grad_keys = (
        jnp.einsum("abwhqk,abwqhe->abwkhe", scores_low, queries, preferred_element_type=jnp.float32)
        * inv_scale
    ).astype(jnp.bfloat16)
    grads_proj = [
        matrix.reshape(-1, local_width) for matrix in (grad_queries, grad_keys, grad_values)
    ]
    grad_qkv_local = jnp.stack(
        [
            jnp.dot(hidden_flat.T, matrix, preferred_element_type=jnp.float32)
            for matrix in grads_proj
        ]
    )
    input_partial = jnp.dot(grads_proj[0], w_qkv[0].T, preferred_element_type=jnp.float32)
    input_partial = input_partial + jnp.dot(
        grads_proj[1], w_qkv[1].T, preferred_element_type=jnp.float32
    )
    input_partial = input_partial + jnp.dot(
        grads_proj[2], w_qkv[2].T, preferred_element_type=jnp.float32
    )
    grad_hidden = lax.psum(input_partial.astype(jnp.bfloat16), "tp")
    grad_own = leave(
        from_windows(grad_hidden.reshape(win_shape)),
        lambda border: passed_along(border, "lon", 1),
        lambda border: passed_along(border, "lat", 1),
    )
    normed, inv_std, unused = layer_norm(latent, ln_gain)
    grad_float = grad_own.astype(jnp.float32)
    scaled = grad_float * ln_gain
    grad_latent = (
        cotangent.astype(jnp.float32)
        + inv_std
        * (
            scaled
            - jnp.mean(scaled, -1, keepdims=True)
            - normed * jnp.mean(scaled * normed, -1, keepdims=True)
        )
    ).astype(jnp.bfloat16)
    gain_local = jnp.sum((grad_float * normed).reshape(-1, model_width), 0)
    grad_wqkv, grad_wout, grad_gain = lax.psum(
        (grad_qkv_local, grad_out_local, gain_local), ("lon", "lat")
    )
    grad_bias = lax.psum(grad_bias_local.astype(jnp.bfloat16), "lon").astype(jnp.float32)
    return (output, grad_latent, grad_gain, grad_wqkv, grad_wout, grad_bias)


def solution(mesh):
    return jax.shard_map(
        on_device,
        mesh=mesh,
        in_specs=(
            P("lon", "lat", None, None),
            P("lon", "lat", None, None),
            P(),
            P(None, None, "tp"),
            P("tp", None),
            P("lat", None, "tp", None),
        ),
        out_specs=(
            P("lon", "lat", None, None),
            P("lon", "lat", None, None),
            P(),
            P(None, None, "tp"),
            P("tp", None),
            P("lat", None, "tp", None),
        ),
        check_vma=False,
    )
```

profile of v0, /device:TPU:0, one launch (start us, length us, event | category | flops | bytes accessed | tf_op | source)
XLA Modules:
  0.0 541.2 jit_solution(10248522876200010188)
XLA Ops:
  7.2 1.4 constant_dynamic-update-slice_fusion.1
  9.0 1.5 fusion.51
  10.5 4.5 collective-permute-start
  15.4 6.9 %copy.66 = f32[2,2,4,3312]{2,1,3,0:T(2,128)} copy(f32[2,2,4,3312]{3,2,1,0:T(4,128)S(1)} %copy-done.31) | data formatting | bytes 423936 | tf_op args[5]
  22.3 78.5 %gather_fusion = f32[20736,2,2,4]{3,2,1,0:T(2,128)} fusion(f32[2,2,4,3312]{2,1,3,0:T(2,128)} %copy.66, s32[21504]{0:T(1024)S(1)} %pad_clamp_fusion), kind=kCustom, calls=%fused_computation | custom fusion | bytes 2737152 | tf_op jit(solution)/shard_map/jit(_take)/gather | solution.py:110
  100.8 59.6 %copy.68 = f32[144,144,2,2,4]{0,1,4,3,2:T(8,128)S(1)} copy(f32[144,144,2,2,4]{4,3,2,1,0:T(2,128)} %bitcast.93) | data formatting | bytes 2654208 | tf_op jit(solution)/shard_map/jit(_take)/gather | solution.py:110
  162.0 1.1 pad_maximum_fusion.5
  163.1 1.6 collective-permute-start.1
  165.3 1.6 fusion.29
  166.9 3.0 collective-permute-done.1
  169.9 1.1 slice_maximum_fusion
  171.0 2.2 fusion.28
  173.2 3.8 reshape.284
  177.1 2.4 copy.59
  180.1 1.3 fusion.17
  184.7 1.0 convolution_convert_fusion.4
  185.7 1.2 slice.112
  186.9 2.1 reshape.316
  189.0 2.1 copy.69
  191.1 2.1 reshape.317
  193.2 2.1 copy.64
  195.3 2.1 reshape.318
  197.4 2.1 copy.65
  199.5 1.8 fusion.1
  201.3 2.5 fusion.54
  204.8 1.1 convolution_convert_fusion.3
  205.9 2.1 reshape.319
  208.0 2.1 copy.75
  210.1 4.0 fusion.10
  214.1 1.8 multiply_reduce_fusion
  215.9 2.1 subtract_multiply_fusion
  218.0 1.1 fusion.13
  219.1 1.3 fusion.12
  220.5 4.1 fusion.11
  224.5 2.5 copy.87
  227.1 1.6 copy.71
  230.3 1.0 reshape.291
  232.2 1.4 fusion.40
  234.6 1.7 copy.85
  236.6 1.4 convolution_add_fusion.1
  238.1 1.3 fusion.7
  239.4 1.0 reshape_reshape.7
  240.5 2.5 copy.86
  243.0 2.8 reshape.297
  245.7 3.0 reshape.298
  248.7 6.8 %copy.88 = f32[20736,16]{1,0:T(8,128)} copy(f32[20736,16]{0,1:T(8,128)} %bitcast.104) | data formatting | bytes 2654208 | tf_op jit(solution)/shard_map/transpose | solution.py:169
  255.6 113.1 %scatter_custom_fusion = f32[3312,16]{1,0:T(8,128)S(1)} fusion(s32[20736]{0:T(1024)} %constant.63, f32[20736,16]{1,0:T(8,128)} %copy.88, f32[]{:T(128)} %constant.17.clone.1), kind=kCustom, calls=%fused_computation.64 | custom fusion | flops 331776 | bytes 212480 | tf_op jit(solution)/shard_map/scatter-add | solution.py:168
  371.5 1.2 fusion.55
  372.8 1.4 slice.113
  374.2 1.7 pad_maximum_fusion.6
  375.9 1.5 collective-permute-start.4
  377.4 1.2 pad_maximum_fusion
  378.7 46.7 %all-reduce.6.cloned.1.call-done = bf16[2,2,4,3312]{3,2,1,0:T(4,128)(2,1)} async-done(((bf16[2,2,4,3312]{3,2,1,0:T(4,128)(2,1)}), bf16[2,2,4,3312]{3,2,1,0:T(4,128)(2,1)}) %all-reduce.6.cloned.1.call-update) | async-done | bytes 106000 | tf_op jit(solution)/shard_map/psum | solution.py:221
  425.4 1.6 convert_element_type.132
  427.5 1.5 collective-permute-start.2
  429.0 1.4 fusion.32
  430.8 1.9 collective-permute-done.2
  433.5 1.3 collective-permute-start.3
  434.8 3.9 collective-permute-done.5
  438.8 1.5 fusion.26
  440.3 31.4 %psum.44 = f32[512]{0:T(512)} all-reduce(f32[512]{0:T(512)S(1)} %get-tuple-element.6), channel_id=1, replica_groups=mesh['lon'=8,'lat'=2,'tp'=2] {'lon','lat'}, use_global_device_ids=true, to_apply=%region_12.13 | all-reduce | flops 512 | bytes 4096 | tf_op jit(solution)/shard_map/psum | solution.py:218
  471.7 2.5 fusion.23
  474.2 56.6 %all-reduce.8.cloned.1.call-done = (f32[3,512,256]{2,1,0:T(8,128)}, f32[256,512]{1,0:T(8,128)}) async-done(((f32[3,512,256]{2,1,0:T(8,128)}, f32[256,512]{1,0:T(8,128)}), (f32[3,512,256]{2,1,0:T(8,128)}, f32[256,512]{1,0:T(8,128)})) %all-reduce.8.cloned.1.call-update) | async-done | bytes 2097168 | tf_op jit(solution)/shard_map/psum | solution.py:218
  530.8 2.7 copy.110
  (126 shorter events, 16.7 us)
Async XLA Ops:
  7.2 197.6 %copy-start = (bf16[256,512]{1,0:T(8,128)(2,1)S(1)}, bf16[256,512]{1,0:T(8,128)(2,1)}, u32[]{:S(2)}) copy-start(bf16[256,512]{1,0:T(8,128)(2,1)} %param.13) | copy-start | bytes 786436
  7.2 1.5 copy-start.22
  7.2 365.6 %all-reduce.10.cloned.1.call-start = ((), (), s32[]{:S(2)}) async-start(), calls=%async_computation.2 | async-start | bytes 2359296 | tf_op jit(solution)/shard_map/psum | solution.py:94
  8.9 6.1 %copy-start.1 = (bf16[12,12,4,512]{3,2,1,0:T(4,128)(2,1)S(1)}, bf16[12,12,4,512]{3,2,1,0:T(4,128)(2,1)}, u32[]{:S(2)}) copy-start(bf16[12,12,4,512]{3,2,1,0:T(4,128)(2,1)} %param.9) | copy-start | bytes 1769476
  9.0 6.4 %copy-start.31 = (f32[2,2,4,3312]{3,2,1,0:T(4,128)S(1)}, f32[2,2,4,3312]{3,2,1,0:T(4,128)}, u32[]{:S(2)}) copy-start(f32[2,2,4,3312]{3,2,1,0:T(4,128)} %param.14) | copy-start | bytes 635908
  10.5 151.5 %collective-permute-start = (bf16[6,12,4,1024]{3,2,1,0:T(4,128)(2,1)}, bf16[6,12,4,1024]{3,2,1,0:T(4,128)(2,1)}, u32[]{:S(2)}, u32[]{:S(2)}) collective-permute-start(bf16[6,12,4,1024]{3,2,1,0:T(4,128)(2,1)} %get-tuple-element.14), channel_id=1, source_target_pairs={{0,28},{4,0},{8,4},{12,8},{16,12},{20,16},{24,20},{28,24},{1,29},{... | collective-permute-start | bytes 1769480 | tf_op jit(solution)/shard_map/ppermute | solution.py:19
  15.3 6.9 %copy-start.32 = (s32[20736]{0:T(1024)S(1)}, s32[20736]{0:T(1024)}, u32[]{:S(2)}) copy-start(s32[20736]{0:T(1024)} %constant.63) | copy-start | bytes 248836
  100.7 59.6 %copy-start.35 = (pred[144]{0:T(512)(128)(4,1)S(1)}, pred[144]{0:T(512)(128)(4,1)}, u32[]{:S(2)}) copy-start(pred[144]{0:T(512)(128)(4,1)} %constant.51.clone) | copy-start | bytes 436
  100.7 59.7 %copy-start.34 = (pred[144]{0:T(512)(128)(4,1)S(1)}, pred[144]{0:T(512)(128)(4,1)}, u32[]{:S(2)}) copy-start(pred[144]{0:T(512)(128)(4,1)} %constant.50.clone) | copy-start | bytes 436
  160.3 1.7 copy-start.9
  163.1 6.8 %collective-permute-start.1 = (bf16[12,3,4,1024]{3,2,1,0:T(4,128)(2,1)S(1)}, bf16[12,3,4,1024]{3,2,1,0:T(4,128)(2,1)S(1)}, u32[]{:S(2)}, u32[]{:S(2)}) collective-permute-start(bf16[12,3,4,1024]{3,2,1,0:T(4,128)(2,1)S(1)} %pad_maximum_fusion.5), channel_id=1, source_target_pairs={{0,2},{2,0},{1,3},{3,1},{4,6},{6,4},{5,7},{7,5},{8,10},{10,8},{9,1... | collective-permute-start | bytes 884744 | tf_op jit(solution)/shard_map/ppermute | solution.py:19
  179.5 2.0 copy-start.33
  181.5 1.1 copy-start.28
  182.5 2.2 copy-start.4
  195.3 4.2 copy-start.29
  201.2 2.6 copy-start.6
  201.2 2.6 copy-start.24
  203.8 10.3 %copy-start.2 = (f32[2,2,4,144,144]{3,4,2,1,0:T(8,128)}, f32[2,2,4,144,144]{3,4,2,1,0:T(8,128)S(1)}, u32[]{:S(2)}) copy-start(f32[2,2,4,144,144]{3,4,2,1,0:T(8,128)S(1)} %get-tuple-element.22) | copy-start | bytes 3981316
  203.9 0.9 copy-start.7
  215.9 2.1 copy-start.11
  218.0 1.1 copy-start.10
  229.0 0.8 copy-start.14
  229.8 1.6 copy-start.26
  232.2 2.0 copy-start.16
  232.2 1.5 copy-start.25
  234.6 3.5 copy-start.20
  236.6 1.5 copy-start.18
  240.4 5.3 copy-start.3
  255.5 169.9 %all-reduce.6.cloned.1.call-start = ((), (), s32[]{:S(2)}) async-start(), calls=%async_computation | async-start | bytes 212992 | tf_op jit(solution)/shard_map/psum | solution.py:221
  368.8 1.1 copy-start.5
  368.8 1.1 copy-start.19
  368.8 1.5 copy-start.21
  369.9 1.0 copy-start.17
  370.3 1.1 copy-start.8
  370.4 1.2 copy-start.15
  372.7 158.1 %all-reduce.8.cloned.1.call-start = ((), (), s32[]{:S(2)}) async-start(), calls=%async_computation.1 | async-start | bytes 4194304 | tf_op jit(solution)/shard_map/psum | solution.py:218
  375.9 53.1 %collective-permute-start.4 = (bf16[12,3,4,512]{3,2,1,0:T(4,128)(2,1)}, bf16[12,3,4,512]{3,2,1,0:T(4,128)(2,1)}, u32[]{:S(2)}, u32[]{:S(2)}) collective-permute-start(bf16[12,3,4,512]{3,2,1,0:T(4,128)(2,1)} %pad_maximum_fusion.6), channel_id=1, source_target_pairs={{0,2},{2,0},{1,3},{3,1},{4,6},{6,4},{5,7},{7,5},{8,10},{10,8},{9,1... | collective-permute-start | bytes 442376 | tf_op jit(solution)/shard_map/ppermute | solution.py:19
  378.7 48.3 %copy-start.12 = (bf16[12,12,4,512]{3,2,1,0:T(4,128)(2,1)S(1)}, bf16[12,12,4,512]{3,2,1,0:T(4,128)(2,1)}, u32[]{:S(2)}) copy-start(bf16[12,12,4,512]{3,2,1,0:T(4,128)(2,1)} %get-tuple-element.11) | copy-start | bytes 1769476
  378.7 50.3 %copy-start.13 = (bf16[12,12,4,512]{3,2,1,0:T(4,128)(2,1)S(1)}, bf16[12,12,4,512]{3,2,1,0:T(4,128)(2,1)}, u32[]{:S(2)}) copy-start(bf16[12,12,4,512]{3,2,1,0:T(4,128)(2,1)} %get-tuple-element.12) | copy-start | bytes 1769476
  427.5 5.2 collective-permute-start.2
  430.7 8.0 %copy-start.27 = (f32[12,12,4]{2,1,0:T(8,128)S(1)}, f32[12,12,4]{2,1,0:T(8,128)}, u32[]{:S(2)}) copy-start(f32[12,12,4]{2,1,0:T(8,128)} %add_rsqrt_fusion.1) | copy-start | bytes 6916
  430.8 8.0 %collective-permute-start.5 = (bf16[6,12,4,512]{3,2,1,0:T(4,128)(2,1)S(1)}, bf16[6,12,4,512]{3,2,1,0:T(4,128)(2,1)S(1)}, u32[]{:S(2)}, u32[]{:S(2)}) collective-permute-start(bf16[6,12,4,512]{3,2,1,0:T(4,128)(2,1)S(1)} %get-tuple-element.17), channel_id=1, source_target_pairs={{0,4},{4,8},{8,12},{12,16},{16,20},{20,24},{24,28},{28,0},{1,5},{5... | collective-permute-start | bytes 884744 | tf_op jit(solution)/shard_map/ppermute | solution.py:19
  433.5 38.2 %copy-start.23 = (bf16[12,12,4,512]{3,2,1,0:T(4,128)(2,1)S(1)}, bf16[12,12,4,512]{3,2,1,0:T(4,128)(2,1)}, u32[]{:S(2)}) copy-start(bf16[12,12,4,512]{3,2,1,0:T(4,128)(2,1)} %param.10) | copy-start | bytes 1769476
  433.5 38.1 %collective-permute-start.3 = (bf16[6,12,4,512]{3,2,1,0:T(4,128)(2,1)S(1)}, bf16[6,12,4,512]{3,2,1,0:T(4,128)(2,1)S(1)}, u32[]{:S(2)}, u32[]{:S(2)}) collective-permute-start(bf16[6,12,4,512]{3,2,1,0:T(4,128)(2,1)S(1)} %get-tuple-element.19), channel_id=1, source_target_pairs={{0,4},{4,8},{8,12},{12,16},{16,20},{20,24},{24,28},{28,0},{1,5},{5... | collective-permute-start | bytes 884744 | tf_op jit(solution)/shard_map/ppermute | solution.py:19
  530.8 2.7 copy-start.30
Sparse Core Ops, SparseCore 0:
  255.7 43.9 all-reduce.9
  372.8 52.5 all-reduce.5
  429.7 101.0 all-reduce.7
where the time goes:
time: 551 us; the launch traced here: 541 us
  local copies, waits for them, and re-layouts  207 us (38%)
  other arithmetic  140 us (25%)
  waiting for transfers between devices  112 us (20%)
  blocking collectives  31.4 us (6%)
  matrix products  25.2 us (5%)
  between operations  14.9 us (3%)
  starting transfers between devices  10.6 us (2%)
    gather x2, local copies, waits for them, and re-layouts, on_device(): bias_full = jnp.take(bias_table, entry_ids, axis=3)  138 us
    scatter-add x1, other arithmetic, on_device(): jax.ops.segment_sum(bias_terms.reshape(-1, WTOK * WTOK).T, entry_ids.resh...  113 us
    psum x1, waiting for transfers between devices, on_device(): lax.psum((grad_qkv_local, grad_out_local, gain_local), ('lon', 'lat'))  56.6 us
    psum x1, waiting for transfers between devices, on_device(): lax.psum(grad_bias_local.astype(jnp.bfloat16), 'lon').astype(jnp.float32)  46.7 us
    psum x1, blocking collectives, on_device(): lax.psum((grad_qkv_local, grad_out_local, gain_local), ('lon', 'lat'))  31.4 us
    another operation x8, local copies, waits for them, and re-layouts  16.7 us
    unnamed x76, local copies, waits for them, and re-layouts  13.5 us
  transfers between devices with their start and end apart: 9, of which 5 were waited for; matrix products, arithmetic and copies ran while one was open for 51% of the time, Pallas kernels for 0%

commit v1 on v0

v1 whole, which is shorter than its diff:
```python
import math

import jax
import jax.numpy as jnp
import numpy as np
from jax import lax
from jax.experimental import pallas as pl
from jax.experimental.pallas import tpu as pltpu
from jax.sharding import PartitionSpec as P

HD = 64
WLON = 12
WLAT = 6
WLEV = 2
WTOK = 144
NREL = 3312
NDIFF = 2 * WLON - 1
CELL = WLAT * WLEV
WIDE = NDIFF * CELL
F32 = jnp.float32
BF16 = jnp.bfloat16


def spread_matrices():
    spread = np.zeros((WLEV, WLAT * NDIFF, WIDE), np.float32)
    for lev in range(WLEV):
        for row in range(WLAT):
            for diff in range(NDIFF):
                spread[lev, row * NDIFF + diff, diff * CELL + lev * WLAT + row] = 1.0
    return spread


def shift_along(shard, lon_by, lat_by):
    lon_count = lax.axis_size("lon")
    lat_count = lax.axis_size("lat")
    pairs = []
    for i in range(lon_count):
        for j in range(lat_count):
            target = ((i + lon_by) % lon_count) * lat_count + (j + lat_by) % lat_count
            pairs.append((i * lat_count + j, target))
    return lax.ppermute(shard, ("lon", "lat"), pairs)


def enter(values):
    lon_half = WLON // 2
    lat_half = WLAT // 2
    corner = shift_along(values[:lon_half, :lat_half], -1, -1)
    lon_part = shift_along(values[:lon_half, lat_half:], -1, 0)
    lat_part = shift_along(values[lon_half:, :lat_half], 0, -1)
    near = jnp.concatenate([values[lon_half:, lat_half:], lat_part], 1)
    far = jnp.concatenate([lon_part, corner], 1)
    values = jnp.concatenate([near, far], 0)
    return jnp.roll(values, -(WLEV // 2), axis=2)


def leave(values):
    lon_half = WLON // 2
    lat_half = WLAT // 2
    values = jnp.roll(values, WLEV // 2, axis=2)
    lon_cut = values.shape[0] - lon_half
    lat_cut = values.shape[1] - lat_half
    corner = shift_along(values[lon_cut:, lat_cut:], 1, 1)
    lon_part = shift_along(values[lon_cut:, :lat_cut], 1, 0)
    lat_part = shift_along(values[:lon_cut, lat_cut:], 0, 1)
    near = jnp.concatenate([corner, lon_part], 1)
    far = jnp.concatenate([lat_part, values[:lon_cut, :lat_cut]], 1)
    return jnp.concatenate([near, far], 0)


def to_windows(values):
    lon_cells, lat_cells, lev_cells, channels = values.shape
    blocks = values.reshape(
        lon_cells // WLON, WLON, lat_cells // WLAT, WLAT, lev_cells // WLEV, WLEV, channels
    )
    blocks = blocks.transpose(2, 4, 0, 1, 5, 3, 6)
    return blocks.reshape(-1, WTOK, channels)


def from_windows(values, lat_bands, lev_bands, lon_bands):
    channels = values.shape[-1]
    blocks = values.reshape(lat_bands, lev_bands, lon_bands, WLON, WLEV, WLAT, channels)
    blocks = blocks.transpose(2, 3, 0, 5, 1, 4, 6)
    return blocks.reshape(lon_bands * WLON, lat_bands * WLAT, lev_bands * WLEV, channels)


def mm(a, b):
    return lax.dot_general(a, b, (((1,), (0,)), ((), ())), preferred_element_type=F32)


def mm_nt(a, b):
    return lax.dot_general(a, b, (((1,), (1,)), ((), ())), preferred_element_type=F32)


def mm_tn(a, b):
    return lax.dot_general(a, b, (((0,), (0,)), ((), ())), preferred_element_type=F32)


def core_kernel(
    head_count,
    lat_ref,
    cot_ref,
    gain_ref,
    wqkv_ref,
    wout_ref,
    table_ref,
    col_ref,
    row_ref,
    out_ref,
    gh_ref,
    gqkv_ref,
    gout_ref,
    gtab_ref,
    hidden_s,
    grads_s,
    att_s,
    cot_s,
    bias_s,
    gtab_s,
):
    step = pl.program_id(0)
    rows = pl.ds(pl.multiple_of(step * WTOK, 16), WTOK)
    inv_scale = 1.0 / math.sqrt(HD)
    width = head_count * HD
    x = lat_ref[0].astype(F32)
    shifted = x - jnp.mean(x, -1, keepdims=True)
    inv_std = lax.rsqrt(jnp.mean(shifted * shifted, -1, keepdims=True) + 1e-05)
    hidden = (shifted * inv_std * gain_ref[...]).astype(BF16)
    hidden_s[rows] = hidden
    cot = cot_ref[0]
    cot_s[rows] = cot
    queries = mm(hidden, wqkv_ref[0]).astype(BF16)
    keys = mm(hidden, wqkv_ref[1]).astype(BF16)
    vals = mm(hidden, wqkv_ref[2]).astype(BF16)
    down = mm_nt(cot, wout_ref[...]).astype(BF16)
    allowed = col_ref[0] == row_ref[0]
    att_parts, gq_parts, gk_parts, gv_parts = [], [], [], []
    for head in range(head_count):
        cols = slice(head * HD, (head + 1) * HD)
        q, k, v, d = queries[:, cols], keys[:, cols], vals[:, cols], down[:, cols]
        table = table_ref[0, head]
        for lon_pos in range(WLON):
            start = (WLON - 1 - lon_pos) * CELL
            bias_s[head, lon_pos * CELL : (lon_pos + 1) * CELL, :] = table[:, start : start + WTOK]
        scores = mm_nt(q, k) * inv_scale + bias_s[head]
        scores = jnp.where(allowed, scores, -jnp.inf)
        expsum = jnp.exp(scores - jnp.max(scores, -1, keepdims=True))
        probs = expsum / jnp.sum(expsum, -1, keepdims=True)
        low = probs.astype(BF16)
        att_parts.append(mm(low, v).astype(BF16))
        dp = mm_nt(d, v)
        gv_parts.append(mm_tn(low, d).astype(BF16))
        ds = probs * (dp - jnp.sum(dp * probs, -1, keepdims=True))
        bias_s[head] = ds
        gtab_s[head] = jnp.zeros((CELL, WIDE), F32)
        for lon_pos in range(WLON):
            start = (WLON - 1 - lon_pos) * CELL
            gtab_s[head, :, start : start + WTOK] += bias_s[
                head, lon_pos * CELL : (lon_pos + 1) * CELL, :
            ]
        gtab_ref[0, head] = gtab_s[head].astype(BF16)
        ds_low = ds.astype(BF16)
        gq_parts.append((mm(ds_low, k) * inv_scale).astype(BF16))
        gk_parts.append((mm_tn(ds_low, q) * inv_scale).astype(BF16))
    att = jnp.concatenate(att_parts, 1)
    att_s[rows] = att
    gq = jnp.concatenate(gq_parts, 1)
    gk = jnp.concatenate(gk_parts, 1)
    gv = jnp.concatenate(gv_parts, 1)
    grads_s[0, rows] = gq
    grads_s[1, rows] = gk
    grads_s[2, rows] = gv
    out_ref[0] = mm(att, wout_ref[...]).astype(BF16)
    gh = mm_nt(gq, wqkv_ref[0])
    gh = gh + mm_nt(gk, wqkv_ref[1])
    gh = gh + mm_nt(gv, wqkv_ref[2])
    gh_ref[0] = gh.astype(BF16)

    @pl.when(step == pl.num_programs(0) - 1)
    def _():
        for member in range(3):
            gqkv_ref[member] = mm_tn(hidden_s[...], grads_s[member]).astype(BF16)
        gout_ref[...] = mm_tn(att_s[...], cot_s[...]).astype(BF16)


def core(lat_win, cot_win, ln_gain, w_qkv, w_out, table, region):
    windows, _, model_width = lat_win.shape
    local_width = w_out.shape[0]
    head_count = local_width // HD
    tokens = windows * WTOK
    whole = lambda *shape: pl.BlockSpec(shape, lambda i: (0,) * len(shape))
    each = lambda *shape: pl.BlockSpec((1,) + shape, lambda i: (i,) + (0,) * len(shape))
    return pl.pallas_call(
        lambda *refs: core_kernel(head_count, *refs),
        grid=(windows,),
        in_specs=[
            each(WTOK, model_width),
            each(WTOK, model_width),
            whole(1, model_width),
            whole(3, model_width, local_width),
            whole(local_width, model_width),
            each(head_count, CELL, WIDE),
            each(WTOK, 1),
            each(1, WTOK),
        ],
        out_specs=[
            each(WTOK, model_width),
            each(WTOK, model_width),
            whole(3, model_width, local_width),
            whole(local_width, model_width),
            each(head_count, CELL, WIDE),
        ],
        out_shape=[
            jax.ShapeDtypeStruct((windows, WTOK, model_width), BF16),
            jax.ShapeDtypeStruct((windows, WTOK, model_width), BF16),
            jax.ShapeDtypeStruct((3, model_width, local_width), BF16),
            jax.ShapeDtypeStruct((local_width, model_width), BF16),
            jax.ShapeDtypeStruct((windows, head_count, CELL, WIDE), BF16),
        ],
        scratch_shapes=[
            pltpu.VMEM((tokens, model_width), BF16),
            pltpu.VMEM((3, tokens, local_width), BF16),
            pltpu.VMEM((tokens, local_width), BF16),
            pltpu.VMEM((tokens, model_width), BF16),
            pltpu.VMEM((head_count, WTOK, WTOK), F32),
            pltpu.VMEM((head_count, CELL, WIDE), F32),
        ],
        compiler_params=pltpu.CompilerParams(vmem_limit_bytes=40 * 1024 * 1024),
        cost_estimate=pl.CostEstimate(
            flops=4 * 10**9, bytes_accessed=8 * 10**6, transcendentals=331776
        ),
    )(lat_win, cot_win, ln_gain.reshape(1, -1), w_qkv, w_out, table, region[:, :, None], region[:, None, :])


def on_device(latent, cotangent, ln_gain, w_qkv, w_out, bias_table):
    lon_cells, lat_cells, lev_cells, model_width = latent.shape
    head_count = w_out.shape[0] // HD
    lat_bands = lat_cells // WLAT
    lev_bands = lev_cells // WLEV
    lon_bands = lon_cells // WLON
    windows = lat_bands * lev_bands * lon_bands
    spread = spread_matrices()

    joined = jnp.concatenate([latent, cotangent], 3)
    rolled = enter(joined)
    lat_win = to_windows(rolled[..., :model_width])
    cot_win = to_windows(rolled[..., model_width:])

    last_device = lax.axis_index("lat") == lax.axis_size("lat") - 1
    position = np.arange(WTOK)
    lat_edge = position % WLAT >= WLAT - WLAT // 2
    lev_edge = position // WLAT % WLEV >= WLEV - WLEV // 2
    lat_last = last_device & (jnp.arange(lat_bands) == lat_bands - 1)
    lev_last = jnp.arange(lev_bands) == lev_bands - 1
    region = (
        2.0 * (lat_last[:, None] & lat_edge).astype(F32)[:, None]
        + (lev_last[:, None] & lev_edge).astype(F32)[None]
    )
    region = jnp.broadcast_to(region[:, :, None], (lat_bands, lev_bands, lon_bands, WTOK))
    region = region.reshape(windows, WTOK)

    grouped = bias_table.reshape(
        lat_bands, lev_bands, head_count, WLEV, WLEV, WLAT, WLAT * NDIFF
    )
    table = sum(
        jnp.einsum(
            "abhtrd,dw->abhtrw", grouped[:, :, :, :, lev], spread[lev], precision=lax.Precision.HIGHEST
        )
        for lev in range(WLEV)
    )
    table = table.reshape(lat_bands * lev_bands, head_count, CELL, WIDE)
    if lon_bands > 1:
        table = jnp.repeat(table, lon_bands, axis=0)

    out_win, gh_win, grad_qkv_local, grad_out_local, grad_tab = core(
        lat_win, cot_win, ln_gain, w_qkv, w_out, table, region
    )
    if lon_bands > 1:
        grad_tab = jnp.sum(
            grad_tab.reshape(lat_bands * lev_bands, lon_bands, head_count, CELL, WIDE).astype(F32), 1
        ).astype(BF16)

    both = lax.psum(jnp.concatenate([out_win, gh_win], -1), "tp")
    both = leave(from_windows(both, lat_bands, lev_bands, lon_bands))
    out_own = both[..., :model_width]
    grad_own = both[..., model_width:]
    output = (latent.astype(F32) + out_own.astype(F32)).astype(BF16)

    values = latent.astype(F32)
    shifted = values - jnp.mean(values, -1, keepdims=True)
    inv_std = lax.rsqrt(jnp.mean(shifted * shifted, -1, keepdims=True) + 1e-05)
    normed = shifted * inv_std
    grad_float = grad_own.astype(F32)
    scaled = grad_float * ln_gain
    grad_latent = (
        cotangent.astype(F32)
        + inv_std
        * (
            scaled
            - jnp.mean(scaled, -1, keepdims=True)
            - normed * jnp.mean(scaled * normed, -1, keepdims=True)
        )
    ).astype(BF16)
    gain_local = jnp.sum((grad_float * normed).reshape(-1, model_width), 0)
    grad_wqkv, grad_wout = lax.psum((grad_qkv_local, grad_out_local), ("lon", "lat"))
    grad_gain = lax.psum(gain_local, ("lon", "lat"))
    grad_tab = lax.psum(grad_tab, "lon")
    grad_tab = grad_tab.reshape(lat_bands, lev_bands, head_count, WLEV, WLAT, WIDE)
    grad_bias = jnp.stack(
        [
            jnp.einsum(
                "abhtrw,dw->abhtrd", grad_tab, spread[lev].astype(BF16), preferred_element_type=F32
            )
            for lev in range(WLEV)
        ],
        axis=4,
    ).reshape(bias_table.shape)
    return (
        output,
        grad_latent,
        grad_gain,
        grad_wqkv.astype(F32),
        grad_wout.astype(F32),
        grad_bias,
    )


def solution(mesh):
    return jax.shard_map(
        on_device,
        mesh=mesh,
        in_specs=(
            P("lon", "lat", None, None),
            P("lon", "lat", None, None),
            P(),
            P(None, None, "tp"),
            P("tp", None),
            P("lat", None, "tp", None),
        ),
        out_specs=(
            P("lon", "lat", None, None),
            P("lon", "lat", None, None),
            P(),
            P(None, None, "tp"),
            P("tp", None),
            P("lat", None, "tp", None),
        ),
        check_vma=False,
    )
```

time: 551 us -> 293 us (0.53); the launches traced: 541 us -> 293 us
  local copies, waits for them, and re-layouts: 207 us -> 18.4 us
  other arithmetic: 140 us -> 14.2 us
  waiting for transfers between devices: 112 us -> 190 us
  matrix products: 25.2 us -> 2.66 us
  Pallas kernels: 0 us -> 13.7 us
    gather x2 -> x0, local copies, waits for them, and re-layouts: 138 us -> none  [on_device(): bias_full = jnp.take(bias_table, entry_ids, axis=3)]
    scatter-add x1 -> x0, other arithmetic: 113 us -> none  [on_device(): jax.ops.segment_sum(bias_terms.reshape(-1, WTOK * WTOK).T, entry_ids.resh...]
    psum x3, waiting for transfers between devices: 103 us -> 186 us  [the longest x1 91.3 us: on_device(): lax.psum((grad_qkv_local, grad_out_local), ('lon', 'lat'))]
    dot_general x18 -> x4, matrix products: 25.2 us -> 2.66 us  [the longest x2 1.46 us: on_device(): jnp.einsum('abhtrw,dw->abhtrd', grad_tab, spread[lev].astype(BF16), prefe...]
    another operation x10 -> x1, local copies, waits for them, and re-layouts: 18 us -> 0.05 us  [on_device(): jnp.stack([jnp.einsum('abhtrw,dw->abhtrd', grad_tab, spread[lev].astype(B...]
    pallas_call x0 -> x1, Pallas kernels: none -> 13.7 us  [core(): pl.pallas_call(lambda *refs: core_kernel(head_count, *refs), grid=(window...]
    unnamed x76 -> x45, local copies, waits for them, and re-layouts: 13.5 us -> 3.12 us
    transpose x3 -> x1, local copies, waits for them, and re-layouts: 9.86 us -> 1.82 us  [from_windows(): blocks = blocks.transpose(2, 3, 0, 5, 1, 4, 6)]
  transfers between devices with their start and end apart: 9 -> 9, of which waited for: 5 -> 5; matrix products, arithmetic and copies ran while one was open for 51% -> 5% of each run, Pallas kernels for 0% -> 0%
where the time goes in v1:
time: 293 us
  waiting for transfers between devices  190 us (65%)
  blocking collectives  31.3 us (11%)
  local copies, waits for them, and re-layouts  18.4 us (6%)
  between operations  14.3 us (5%)
  other arithmetic  14.2 us (5%)
  Pallas kernels  13.7 us (5%)
  starting transfers between devices  8.12 us (3%)
    psum x1, waiting for transfers between devices, on_device(): lax.psum((grad_qkv_local, grad_out_local), ('lon', 'lat'))  91.3 us
    psum x1, waiting for transfers between devices, on_device(): grad_tab = lax.psum(grad_tab, 'lon')  55 us
    psum x1, waiting for transfers between devices, on_device(): both = lax.psum(jnp.concatenate([out_win, gh_win], -1), 'tp')  39.9 us
    psum x1, blocking collectives, on_device(): grad_gain = lax.psum(gain_local, ('lon', 'lat'))  31.3 us
    pallas_call x1, Pallas kernels, core(): pl.pallas_call(lambda *refs: core_kernel(head_count, *refs), grid=(window...  13.7 us
    ppermute x6, starting transfers between devices, shift_along(): return lax.ppermute(shard, ('lon', 'lat'), pairs)  8 us
  transfers between devices with their start and end apart: 9, of which 5 were waited for; matrix products, arithmetic and copies ran while one was open for 5% of the time, Pallas kernels for 0%

profile of v1, /device:TPU:0, one launch (start us, length us, event | category | flops | bytes accessed | tf_op | source)
XLA Modules:
  0.0 293.0 jit_solution(15568834577857720807)
XLA Ops:
  7.2 0.0 all-reduce.5.cloned.1.call-start
  7.2 1.4 constant_dynamic-update-slice_fusion.1
  8.6 0.3 constant_dynamic-update-slice_fusion
  8.9 0.4 fusion.21
  9.3 4.5 %collective-permute-start.1 = (bf16[6,9,4,1024]{3,2,1,0:T(4,128)(2,1)S(1)}, bf16[6,9,4,1024]{3,2,1,0:T(4,128)(2,1)S(1)}, u32[]{:S(2)}, u32[]{:S(2)}) collective-permute-start(bf16[6,9,4,1024]{3,2,1,0:T(4,128)(2,1)S(1)} %get-tuple-element.28), channel_id=1, source_target_pairs={{0,28},{2,30},{4,0},{6,2},{8,4},{10,6},{12,8},{14,10},{16,12},{18,... | collective-permute-start | bytes 1327112 | tf_op jit(solution)/shard_map/ppermute | solution.py:41
  13.9 0.1 fusion.22
  14.0 1.6 collective-permute-start
  15.6 0.3 collective-permute-start.2
  15.9 0.1 and_select_fusion
  16.0 0.1 and_convert_fusion
  16.1 0.2 add.74.refs_6_
  16.4 0.5 reshape.177
  16.9 0.6 fusion.19
  17.5 0.6 fusion.6
  18.1 0.1 copy.38
  18.3 3.2 %collective-permute-done = bf16[6,3,4,1024]{3,2,1,0:T(4,128)(2,1)S(1)} collective-permute-done((bf16[6,3,4,1024]{3,2,1,0:T(4,128)(2,1)S(1)}, bf16[6,3,4,1024]{3,2,1,0:T(4,128)(2,1)S(1)}, u32[]{:S(2)}, u32[]{:S(2)}) %collective-permute-start) | collective-permute-done | bytes 147488 | tf_op jit(solution)/shard_map/ppermute | solution.py:41
  21.4 0.9 collective-permute-done.2
  22.4 0.8 maximum_maximum_fusion
  23.2 0.7 slice.80
  23.9 0.5 slice.81
  24.4 1.2 pad_maximum_fusion.2
  25.6 0.2 reshape.172
  25.9 0.5 copy.57
  26.4 0.2 reshape.173
  26.6 0.1 copy.39.refs_0_
  26.7 0.2 reshape.174
  27.0 0.5 copy.56
  27.5 1.0 reshape.175
  28.6 1.2 copy.40.refs_1_
  29.8 13.7 %shard_map.163 = (bf16[4,144,512]{2,1,0:T(8,128)(2,1)S(1)}, bf16[4,144,512]{2,1,0:T(8,128)(2,1)S(1)}, bf16[3,512,256]{2,1,0:T(8,128)(2,1)}, bf16[256,512]{1,0:T(8,128)(2,1)}, bf16[4,4,12,276]{3,2,1,0:T(8,128)(2,1)S(1)}) custom-call(bf16[4,144,512]{2,1,0:T(8,128)(2,1)S(1)} %copy.39.refs_0_, bf16[4,144,512]{2,1,0:T(8,128)(2,1)S(1)} %copy.40.refs_1_, ...), custom_call_target="tpu_custom_call" | custom-call | flops 4000000000 | bytes 8000000 | tf_op jit(solution)/shard_map/pallas_call | solution.py:192
  43.5 0.2 pad_maximum_fusion.1
  43.6 0.9 copy.43
  44.6 0.5 reshape.179
  45.1 1.8 copy.44
  46.9 1.3 reshape.180
  48.2 0.0 all-reduce.7.cloned.1.call-start
  48.3 1.0 copy-done.3
  49.3 0.3 convert_reduce_fusion
  49.6 0.6 fusion.11
  50.2 0.1 copy.45
  50.3 0.7 copy.46
  51.0 0.0 all-reduce.9.cloned.1.call-start
  51.1 0.7 add_rsqrt_fusion
  51.7 0.0 all-reduce.9.cloned.1.call-update
  51.7 39.9 %all-reduce.5.cloned.1.call-done = bf16[12,12,4,1024]{3,2,1,0:T(4,128)(2,1)} async-done(((bf16[12,12,4,1024]{3,2,1,0:T(4,128)(2,1)}), bf16[12,12,4,1024]{3,2,1,0:T(4,128)(2,1)}) %all-reduce.5.cloned.1.call-update) | async-done | bytes 1179664 | tf_op jit(solution)/shard_map/psum | solution.py:282
  91.6 2.1 slice.86
  93.7 0.5 fusion.18
  94.2 0.1 collective-permute-start.4
  94.2 55.0 %all-reduce.7.cloned.1.call-done = bf16[2,2,4,2,6,276]{5,4,3,2,1,0:T(8,128)(2,1)} async-done(((bf16[2,2,4,2,6,276]{5,4,3,2,1,0:T(8,128)(2,1)}), bf16[2,2,4,2,6,276]{5,4,3,2,1,0:T(8,128)(2,1)}) %all-reduce.7.cloned.1.call-update) | async-done | bytes 106000 | tf_op jit(solution)/shard_map/psum | solution.py:306
  149.3 1.2 convolution_bitcast_fusion
  150.5 1.0 pad_maximum_fusion.4
  151.5 1.5 collective-permute-start.5
  153.0 0.2 convolution_bitcast_fusion.1
  153.2 0.1 pad_maximum_fusion.3
  153.3 0.1 copy.47
  153.4 1.0 reshape.182
  154.4 91.3 %all-reduce.9.cloned.1.call-done = (bf16[3,512,256]{2,1,0:T(8,128)(2,1)}, bf16[256,512]{1,0:T(8,128)(2,1)}) async-done(((bf16[3,512,256]{2,1,0:T(8,128)(2,1)}, bf16[256,512]{1,0:T(8,128)(2,1)}), (bf16[3,512,256]{2,1,0:T(8,128)(2,1)}, bf16[256,512]{1,0:T(8,128)(2,1)})) %all-reduce.9.cloned.1.call-update) | async-done | bytes 1048592 | tf_op jit(solution)/shard_map/psum | solution.py:304
  245.7 2.4 convert_element_type.41
  248.1 0.9 convert_element_type.42
  249.0 0.7 copy-done.15
  249.7 1.9 fusion.16
  251.7 1.4 fusion.13
  253.1 31.3 %psum.36 = f32[512]{0:T(512)} all-reduce(f32[512]{0:T(512)S(1)} %get-tuple-element.16), channel_id=1, replica_groups=mesh['lon'=8,'lat'=2,'tp'=2] {'lon','lat'}, use_global_device_ids=true, to_apply=%region_6.7 | all-reduce | flops 512 | bytes 4096 | tf_op jit(solution)/shard_map/psum | solution.py:305
  284.4 2.1 fusion.10
  (56 shorter events, 0.3 us)
Async XLA Ops:
  7.2 1.4 copy-start.5
  7.2 84.4 %all-reduce.5.cloned.1.call-start = ((), (), s32[]{:S(2)}) async-start(), calls=%async_computation | async-start | bytes 2359296 | tf_op jit(solution)/shard_map/psum | solution.py:282
  8.9 7.0 %copy-start.19 = (pred[144]{0:T(512)(128)(4,1)S(1)}, pred[144]{0:T(512)(128)(4,1)}, u32[]{:S(2)}) copy-start(pred[144]{0:T(512)(128)(4,1)} %constant.32.clone) | copy-start | bytes 436
  8.9 7.1 %copy-start.18 = (pred[144]{0:T(512)(128)(4,1)S(1)}, pred[144]{0:T(512)(128)(4,1)}, u32[]{:S(2)}) copy-start(pred[144]{0:T(512)(128)(4,1)} %constant.33.clone) | copy-start | bytes 436
  8.9 7.4 %copy-start.14 = (f32[2,2,4,3312]{3,2,1,0:T(4,128)S(1)}, f32[2,2,4,3312]{3,2,1,0:T(4,128)}, u32[]{:S(2)}) copy-start(f32[2,2,4,3312]{3,2,1,0:T(4,128)} %param.17) | copy-start | bytes 635908
  9.3 7.5 %copy-start.21 = (f32[138,276,1,1,1,1]{1,0,5,4,3,2:T(8,128)S(1)}, f32[138,276,1,1,1,1]{1,0,5,4,3,2:T(8,128)}, u32[]{:S(2)}) copy-start(f32[138,276,1,1,1,1]{1,0,5,4,3,2:T(8,128)} %constant.40) | copy-start | bytes 457060
  9.3 13.0 %collective-permute-start.1 = (bf16[6,9,4,1024]{3,2,1,0:T(4,128)(2,1)S(1)}, bf16[6,9,4,1024]{3,2,1,0:T(4,128)(2,1)S(1)}, u32[]{:S(2)}, u32[]{:S(2)}) collective-permute-start(bf16[6,9,4,1024]{3,2,1,0:T(4,128)(2,1)S(1)} %get-tuple-element.28), channel_id=1, source_target_pairs={{0,28},{2,30},{4,0},{6,2},{8,4},{10,6},{12,8},{14,10},{16,12},{18,... | collective-permute-start | bytes 1327112 | tf_op jit(solution)/shard_map/ppermute | solution.py:41
  14.0 7.4 %collective-permute-start = (bf16[6,3,4,1024]{3,2,1,0:T(4,128)(2,1)S(1)}, bf16[6,3,4,1024]{3,2,1,0:T(4,128)(2,1)S(1)}, u32[]{:S(2)}, u32[]{:S(2)}) collective-permute-start(bf16[6,3,4,1024]{3,2,1,0:T(4,128)(2,1)S(1)} %get-tuple-element.29), channel_id=1, source_target_pairs={{0,2},{2,0},{4,6},{6,4},{8,10},{10,8},{12,14},{14,12},{16,18},{18,... | collective-permute-start | bytes 442376 | tf_op jit(solution)/shard_map/ppermute | solution.py:41
  15.6 6.8 %collective-permute-start.2 = (bf16[6,3,4,1024]{3,2,1,0:T(4,128)(2,1)S(1)}, bf16[6,3,4,1024]{3,2,1,0:T(4,128)(2,1)S(1)}, u32[]{:S(2)}, u32[]{:S(2)}) collective-permute-start(bf16[6,3,4,1024]{3,2,1,0:T(4,128)(2,1)S(1)} %get-tuple-element.30), channel_id=1, source_target_pairs={{0,30},{2,28},{4,2},{6,0},{8,6},{10,4},{12,10},{14,8},{16,14},{18,... | collective-permute-start | bytes 442376 | tf_op jit(solution)/shard_map/ppermute | solution.py:41
  16.3 1.1 copy-start.20
  27.5 2.2 copy-start
  27.5 2.2 copy-start.1
  27.5 2.2 copy-start.2
  48.2 1.1 copy-start.3
  48.2 101.0 %all-reduce.7.cloned.1.call-start = ((), (), s32[]{:S(2)}) async-start(), calls=%async_computation.1 | async-start | bytes 393216 | tf_op jit(solution)/shard_map/psum | solution.py:306
  49.6 0.7 copy-start.7
  51.0 194.7 %all-reduce.9.cloned.1.call-start = ((), (), s32[]{:S(2)}) async-start(), calls=%async_computation.2 | async-start | bytes 2097152 | tf_op jit(solution)/shard_map/psum | solution.py:304
  91.6 2.1 copy-start.4
  93.7 55.6 %copy-start.17 = (bf16[138,276,1,1,1,1]{1,0,5,4,3,2:T(8,128)(2,1)S(1)}, bf16[138,276,1,1,1,1]{1,0,5,4,3,2:T(8,128)(2,1)}, u32[]{:S(2)}) copy-start(bf16[138,276,1,1,1,1]{1,0,5,4,3,2:T(8,128)(2,1)} %constant.43) | copy-start | bytes 228532
  94.2 58.8 %copy-start.16 = (bf16[138,276,1,1,1,1]{1,0,5,4,3,2:T(8,128)(2,1)S(1)}, bf16[138,276,1,1,1,1]{1,0,5,4,3,2:T(8,128)(2,1)}, u32[]{:S(2)}) copy-start(bf16[138,276,1,1,1,1]{1,0,5,4,3,2:T(8,128)(2,1)} %constant.42) | copy-start | bytes 228532
  94.2 155.5 %collective-permute-start.4 = (bf16[6,9,4,1024]{3,2,1,0:T(4,128)(2,1)S(1)}, bf16[6,9,4,1024]{3,2,1,0:T(4,128)(2,1)}, u32[]{:S(2)}, u32[]{:S(2)}) collective-permute-start(bf16[6,9,4,1024]{3,2,1,0:T(4,128)(2,1)S(1)} %fusion.18), channel_id=1, source_target_pairs={{0,4},{2,6},{4,8},{6,10},{8,12},{10,14},{12,16},{14,18},{16,20},{1... | collective-permute-start | bytes 1327112 | tf_op jit(solution)/shard_map/ppermute | solution.py:41
  149.3 3.7 %copy-start.12 = (bf16[2,2,4,2,6,276]{5,4,3,2,1,0:T(8,128)(2,1)S(1)}, bf16[2,2,4,2,6,276]{5,4,3,2,1,0:T(8,128)(2,1)}, u32[]{:S(2)}) copy-start(bf16[2,2,4,2,6,276]{5,4,3,2,1,0:T(8,128)(2,1)} %all-reduce.7.cloned.1.call-done) | copy-start | bytes 317956
  151.5 97.5 %collective-permute-start.3 = (bf16[6,3,4,1024]{3,2,1,0:T(4,128)(2,1)}, bf16[6,3,4,1024]{3,2,1,0:T(4,128)(2,1)}, u32[]{:S(2)}, u32[]{:S(2)}) collective-permute-start(bf16[6,3,4,1024]{3,2,1,0:T(4,128)(2,1)} %get-tuple-element.23), channel_id=1, source_target_pairs={{0,6},{2,4},{4,10},{6,8},{8,14},{10,12},{12,18},{14,16},{16,22},{1... | collective-permute-start | bytes 442376 | tf_op jit(solution)/shard_map/ppermute | solution.py:41
  151.5 97.5 %collective-permute-start.5 = (bf16[6,3,4,1024]{3,2,1,0:T(4,128)(2,1)}, bf16[6,3,4,1024]{3,2,1,0:T(4,128)(2,1)S(1)}, u32[]{:S(2)}, u32[]{:S(2)}) collective-permute-start(bf16[6,3,4,1024]{3,2,1,0:T(4,128)(2,1)} %get-tuple-element.24), channel_id=1, source_target_pairs={{0,2},{2,0},{4,6},{6,4},{8,10},{10,8},{12,14},{14,12},{16,18},{18,... | collective-permute-start | bytes 442376 | tf_op jit(solution)/shard_map/ppermute | solution.py:41
  245.7 2.5 copy-start.13
  249.0 2.6 copy-start.8
  249.0 2.6 copy-start.10
  249.0 0.7 copy-start.15
  251.6 32.8 %copy-start.6 = (bf16[12,12,4,512]{3,2,1,0:T(4,128)(2,1)S(1)}, bf16[12,12,4,512]{3,2,1,0:T(4,128)(2,1)}, u32[]{:S(2)}) copy-start(bf16[12,12,4,512]{3,2,1,0:T(4,128)(2,1)} %param.13) | copy-start | bytes 1769476
  251.6 32.8 %copy-start.9 = (f32[12,12,4]{2,1,0:T(8,128)S(1)}, f32[12,12,4]{2,1,0:T(8,128)}, u32[]{:S(2)}) copy-start(f32[12,12,4]{2,1,0:T(8,128)} %copy-done.7) | copy-start | bytes 6916
  251.7 32.8 %copy-start.11 = (f32[12,12,4]{2,1,0:T(8,128)S(1)}, f32[12,12,4]{2,1,0:T(8,128)}, u32[]{:S(2)}) copy-start(f32[12,12,4]{2,1,0:T(8,128)} %add_rsqrt_fusion) | copy-start | bytes 6916
Sparse Core Ops, SparseCore 0:
  48.3 43.2 all-reduce.4
  94.6 54.6 all-reduce.6
  153.4 92.2 all-reduce.8

commit v2 on v1

v2 whole, which is shorter than its diff:
```python
import math

import jax
import jax.numpy as jnp
import numpy as np
from jax import lax
from jax.experimental import pallas as pl
from jax.experimental.pallas import tpu as pltpu
from jax.sharding import PartitionSpec as P

HD = 64
WLON = 12
WLAT = 6
WLEV = 2
WTOK = 144
NREL = 3312
NDIFF = 2 * WLON - 1
CELL = WLAT * WLEV
WIDE = NDIFF * CELL
F32 = jnp.float32
BF16 = jnp.bfloat16


def spread_matrices():
    spread = np.zeros((WLEV, WLAT * NDIFF, WIDE), np.float32)
    for lev in range(WLEV):
        for row in range(WLAT):
            for diff in range(NDIFF):
                spread[lev, row * NDIFF + diff, diff * CELL + lev * WLAT + row] = 1.0
    return spread


def mm(a, b):
    return lax.dot_general(a, b, (((1,), (0,)), ((), ())), preferred_element_type=F32)


def mm_nt(a, b):
    return lax.dot_general(a, b, (((1,), (1,)), ((), ())), preferred_element_type=F32)


def mm_tn(a, b):
    return lax.dot_general(a, b, (((0,), (0,)), ((), ())), preferred_element_type=F32)


def round_up(count, to):
    return -(-count // to) * to


def halo_layout(lon_cells, lat_cells, lev_cells):
    lon_half, lat_half, lev_half = WLON // 2, WLAT // 2, WLEV // 2
    tokens = lon_cells * lat_cells * lev_cells
    cells = np.arange(tokens).reshape(lon_cells, lat_cells, lev_cells)
    pieces = [
        cells[:lon_half, lat_half:],
        cells[lon_half:, :lat_half],
        cells[:lon_half, :lat_half],
    ]
    starts, total = [], 0
    for piece in pieces:
        starts.append((total, round_up(piece.size, 16)))
        total += round_up(piece.size, 16)
    gather = np.zeros((total, tokens), np.float32)
    slots = []
    for piece, (start, _) in zip(pieces, starts):
        gather[start + np.arange(piece.size), piece.reshape(-1)] = 1.0
        slots.append(tokens + start + np.arange(piece.size).reshape(piece.shape))
    near = np.concatenate([cells[lon_half:, lat_half:], slots[1]], 1)
    far = np.concatenate([slots[0], slots[2]], 1)
    rolled = np.roll(np.concatenate([near, far], 0), -lev_half, axis=2)
    lonb, latb, levb = lon_cells // WLON, lat_cells // WLAT, lev_cells // WLEV
    order = rolled.reshape(lonb, WLON, latb, WLAT, levb, WLEV)
    order = order.transpose(2, 4, 0, 1, 5, 3).reshape(-1)
    place = np.zeros((tokens, tokens + total), np.float32)
    place[np.arange(tokens), order] = 1.0
    return gather, place[:, :tokens], place[:, tokens:], starts


def fused_kernel(
    cfg,
    x_ref,
    gain_ref,
    wqkv_ref,
    wout_ref,
    table_ref,
    col_ref,
    row_ref,
    gather_ref,
    own_ref,
    arrived_ref,
    gather_t_ref,
    own_t_ref,
    arrived_t_ref,
    out_ref,
    glat_ref,
    gqkv_ref,
    gout_ref,
    gtab_ref,
    ggain_ref,
    pack_s,
    halo_s,
    back_s,
    win_s,
    hidden_s,
    grads_s,
    att_s,
    bias_s,
    gtab_s,
    mine_s,
    theirs_s,
    wg_s,
    wg_core,
    wg_a,
    wg_lat,
    wg_b,
    wg_z,
    wg_zg,
    wg_lg,
    wg_cg,
    tab_s,
    tab_core,
    tab_a,
    tab_z,
    tab_zg,
    tab_cg,
    gain_s,
    in_send,
    in_recv,
    tp_send,
    tp_recv,
    out_send,
    out_recv,
    core_send,
    core_recv,
    lat_send,
    lat_recv,
    z_send,
    z_recv,
    tz_send,
    tz_recv,
    gain_send,
    gain_recv,
):
    heads, windows, starts, n_lon, n_lat, n_tp = cfg
    n_z = n_lon // 2
    model_width = gain_ref.shape[1]
    inv_scale = 1.0 / math.sqrt(HD)
    lon, lat, tp = lax.axis_index("lon"), lax.axis_index("lat"), lax.axis_index("tp")
    z, core = lax.div(lon, 2), lax.rem(lon, 2)
    sibling = lon + 1 - 2 * core
    group = lat * n_tp + tp

    def device(lon_at, lat_at, tp_at):
        return {"lon": lon_at, "lat": lat_at, "tp": tp_at}

    def send(src, dst, send_sem, recv_sem, where):
        return pltpu.make_async_remote_copy(
            src_ref=src,
            dst_ref=dst,
            send_sem=send_sem,
            recv_sem=recv_sem,
            device_id=where,
            device_id_type=pl.DeviceIdType.MESH,
        )

    lon_next, lon_prev = lax.rem(lon + 1, n_lon), lax.rem(lon + n_lon - 1, n_lon)
    lat_next, lat_prev = lax.rem(lat + 1, n_lat), lax.rem(lat + n_lat - 1, n_lat)
    before = [
        device(lon_prev, lat, tp),
        device(lon, lat_prev, tp),
        device(lon_prev, lat_prev, tp),
    ]
    after = [
        device(lon_next, lat, tp),
        device(lon, lat_next, tp),
        device(lon_next, lat_next, tp),
    ]
    z_peers = [device(lax.rem(z + d, n_z) * 2 + core, lat, tp) for d in range(1, n_z)]
    lat_peers = [device(lon, lax.rem(lat + d, n_lat), tp) for d in range(1, n_lat)]
    group_peers = []
    for d in range(1, n_lat * n_tp):
        other = lax.rem(group + d, n_lat * n_tp)
        group_peers.append(device(lon, lax.div(other, n_tp), lax.rem(other, n_tp)))
    core_peer = device(sibling, lat, tp)
    tp_peer = device(lon, lat, lax.rem(tp + 1, n_tp))

    barrier = pltpu.get_barrier_semaphore()
    greeted = before + after + z_peers + group_peers + [core_peer]
    for where in greeted:
        pl.semaphore_signal(
            barrier, inc=1, device_id=where, device_id_type=pl.DeviceIdType.MESH
        )
    pack_s[...] = mm(gather_ref[...], x_ref[...]).astype(BF16)
    pl.semaphore_wait(barrier, len(greeted))
    halo = [
        send(
            pack_s.at[pl.ds(start, size)],
            halo_s.at[pl.ds(start, size)],
            in_send.at[i],
            in_recv.at[i],
            before[i],
        )
        for i, (start, size) in enumerate(starts)
    ]
    for copy in halo:
        copy.start()
    win_s[...] = mm(own_ref[...], x_ref[...]).astype(BF16)
    for copy in halo:
        copy.wait()
    win_s[...] += mm(arrived_ref[...], halo_s[...]).astype(BF16)

    gain_s[group] = jnp.zeros(gain_s.shape[1:], F32)

    def tp_copy(w):
        rows = pl.ds(pl.multiple_of(w * WTOK, 16), WTOK)
        return send(mine_s.at[rows], theirs_s.at[rows], tp_send.at[w], tp_recv.at[w], tp_peer)

    def window(w, carry):
        rows = pl.ds(pl.multiple_of(w * WTOK, 16), WTOK)
        x = win_s[rows, :model_width].astype(F32)
        cot = win_s[rows, model_width:]
        shifted = x - jnp.mean(x, -1, keepdims=True)
        inv_std = lax.rsqrt(jnp.mean(shifted * shifted, -1, keepdims=True) + 1e-05)
        normed = shifted * inv_std
        hidden = (normed * gain_ref[...]).astype(BF16)
        hidden_s[rows] = hidden
        queries = mm(hidden, wqkv_ref[0]).astype(BF16)
        keys = mm(hidden, wqkv_ref[1]).astype(BF16)
        vals = mm(hidden, wqkv_ref[2]).astype(BF16)
        down = mm_nt(cot, wout_ref[...]).astype(BF16)
        allowed = col_ref[w] == row_ref[w]
        att_parts, gq_parts, gk_parts, gv_parts = [], [], [], []
        for head in range(heads):
            cols = slice(head * HD, (head + 1) * HD)
            q, k, v, d = queries[:, cols], keys[:, cols], vals[:, cols], down[:, cols]
            table = table_ref[w, head]
            for lon_pos in range(WLON):
                start = (WLON - 1 - lon_pos) * CELL
                bias_s[head, lon_pos * CELL : (lon_pos + 1) * CELL, :] = table[
                    :, start : start + WTOK
                ]
            scores = mm_nt(q, k) * inv_scale + bias_s[head]
            scores = jnp.where(allowed, scores, -jnp.inf)
            expsum = jnp.exp(scores - jnp.max(scores, -1, keepdims=True))
            probs = expsum / jnp.sum(expsum, -1, keepdims=True)
            low = probs.astype(BF16)
            att_parts.append(mm(low, v).astype(BF16))
            dp = mm_nt(d, v)
            gv_parts.append(mm_tn(low, d).astype(BF16))
            ds = probs * (dp - jnp.sum(dp * probs, -1, keepdims=True))
            bias_s[head] = ds
            gtab_s[head] = jnp.zeros(gtab_s.shape[1:], F32)
            for lon_pos in range(WLON):
                start = (WLON - 1 - lon_pos) * CELL
                gtab_s[head, :CELL, start : start + WTOK] += bias_s[
                    head, lon_pos * CELL : (lon_pos + 1) * CELL, :
                ]
            block = pl.ds(pl.multiple_of((w * heads + head) * 16, 16), 16)
            tab_s[block] = gtab_s[head].astype(BF16)
            ds_low = ds.astype(BF16)
            gq_parts.append((mm(ds_low, k) * inv_scale).astype(BF16))
            gk_parts.append((mm_tn(ds_low, q) * inv_scale).astype(BF16))
        att = jnp.concatenate(att_parts, 1)
        att_s[rows] = att
        gq = jnp.concatenate(gq_parts, 1)
        gk = jnp.concatenate(gk_parts, 1)
        gv = jnp.concatenate(gv_parts, 1)
        grads_s[0, rows] = gq
        grads_s[1, rows] = gk
        grads_s[2, rows] = gv
        mine_s[rows, :model_width] = mm(att, wout_ref[...]).astype(BF16)
        gh = mm_nt(gq, wqkv_ref[0])
        gh = gh + mm_nt(gk, wqkv_ref[1])
        gh = (gh + mm_nt(gv, wqkv_ref[2])).astype(BF16)
        mine_s[rows, model_width:] = gh
        tp_copy(w).start()
        gain_s[group, 0:1] += jnp.sum(gh.astype(F32) * normed, 0, keepdims=True)
        return carry

    lax.fori_loop(0, windows, window, 0)

    gain_copies = [
        send(gain_s.at[group], gain_s.at[group], gain_send.at[i], gain_recv.at[i], where)
        for i, where in enumerate(group_peers)
    ]
    for copy in gain_copies:
        copy.start()

    local_width = wout_ref.shape[0]
    for member in range(3):
        wg_s[member * model_width : (member + 1) * model_width] = mm_tn(
            hidden_s[...], grads_s[member]
        ).astype(BF16)
    gout = mm_tn(att_s[...], win_s[:, model_width:]).astype(BF16)
    out_parts = model_width // local_width
    for part in range(out_parts):
        first = 3 * model_width + part * local_width
        wg_s[first : first + local_width] = gout[:, part * local_width : (part + 1) * local_width]

    half = wg_s.shape[0] // 2
    tab_half = tab_s.shape[0] // 2
    wg_mine = pl.ds(pl.multiple_of(core * half, 16), half)
    wg_other = pl.ds(pl.multiple_of((1 - core) * half, 16), half)
    tab_mine = pl.ds(pl.multiple_of(core * tab_half, 16), tab_half)
    tab_other = pl.ds(pl.multiple_of((1 - core) * tab_half, 16), tab_half)

    wg_copy = send(wg_s.at[wg_other], wg_core, core_send.at[0], core_recv.at[0], core_peer)
    wg_copy.start()

    for copy in gain_copies:
        copy.wait()
    gain_total = gain_s[0, 0:1]
    for i in range(1, n_lat * n_tp):
        gain_total = gain_total + gain_s[i, 0:1]
    tab_width = tab_s.shape[1]
    spare = jnp.concatenate(
        [gain_total, jnp.zeros((1, 2 * tab_width - model_width), F32)], 1
    )
    gtab_s[0] = tab_s[0:16].astype(F32)
    gtab_s[0, CELL : CELL + 1] = spare[:, :tab_width]
    gtab_s[0, CELL + 1 : CELL + 2] = spare[:, tab_width:]
    tab_s[0:16] = gtab_s[0].astype(BF16)
    tab_copy = send(tab_s.at[tab_other], tab_core, core_send.at[1], core_recv.at[1], core_peer)
    tab_copy.start()

    wg_copy.wait()
    wg_a[...] = (wg_s[wg_mine].astype(F32) + wg_core[...].astype(F32)).astype(BF16)
    part = half // n_lat
    lat_copies = [
        send(
            wg_a.at[pl.ds(pl.multiple_of(lax.rem(lat + d, n_lat) * part, 16), part)],
            wg_lat.at[d - 1],
            lat_send.at[d - 1],
            lat_recv.at[d - 1],
            lat_peers[d - 1],
        )
        for d in range(1, n_lat)
    ]
    for copy in lat_copies:
        copy.start()
    tab_copy.wait()
    tab_a[...] = (tab_s[tab_mine].astype(F32) + tab_core[...].astype(F32)).astype(BF16)
    tab_piece = tab_half // n_z
    tabz_copies = [
        send(
            tab_a.at[pl.ds(pl.multiple_of(lax.rem(z + d, n_z) * tab_piece, 16), tab_piece)],
            tab_z.at[d - 1],
            tz_send.at[d - 1],
            tz_recv.at[d - 1],
            z_peers[d - 1],
        )
        for d in range(1, n_z)
    ]
    for copy in tabz_copies:
        copy.start()
    for copy in lat_copies:
        copy.wait()
    total = wg_a[pl.ds(pl.multiple_of(lat * part, 16), part)].astype(F32)
    for d in range(1, n_lat):
        total = total + wg_lat[d - 1].astype(F32)
    wg_b[...] = total.astype(BF16)
    piece = part // n_z
    z_copies = [
        send(
            wg_b.at[pl.ds(pl.multiple_of(lax.rem(z + d, n_z) * piece, 16), piece)],
            wg_z.at[d - 1],
            z_send.at[d - 1],
            z_recv.at[d - 1],
            z_peers[d - 1],
        )
        for d in range(1, n_z)
    ]
    for copy in z_copies:
        copy.start()
    for copy in tabz_copies:
        copy.wait()
    tab_rows = pl.ds(pl.multiple_of(z * tab_piece, 16), tab_piece)
    total = tab_a[tab_rows].astype(F32)
    for d in range(1, n_z):
        total = total + tab_z[d - 1].astype(F32)
    tab_zg[tab_rows] = total.astype(BF16)
    tabg_copies = [
        send(
            tab_zg.at[tab_rows],
            tab_zg.at[tab_rows],
            tz_send.at[n_z - 1 + d - 1],
            tz_recv.at[n_z - 1 + d - 1],
            z_peers[d - 1],
        )
        for d in range(1, n_z)
    ]
    for copy in tabg_copies:
        copy.start()

    def arrive(w, carry):
        tp_copy(w).wait()
        return carry

    lax.fori_loop(0, windows, arrive, 0)
    win_s[...] = (mine_s[...].astype(F32) + theirs_s[...].astype(F32)).astype(BF16)
    pack_s[...] = mm(arrived_t_ref[...], win_s[...]).astype(BF16)
    back = [
        send(
            pack_s.at[pl.ds(start, size)],
            back_s.at[pl.ds(start, size)],
            out_send.at[i],
            out_recv.at[i],
            after[i],
        )
        for i, (start, size) in enumerate(starts)
    ]
    for copy in back:
        copy.start()

    for copy in z_copies:
        copy.wait()
    z_rows = pl.ds(pl.multiple_of(z * piece, 16), piece)
    total = wg_b[z_rows].astype(F32)
    for d in range(1, n_z):
        total = total + wg_z[d - 1].astype(F32)
    wg_zg[z_rows] = total.astype(BF16)
    zg_copies = [
        send(
            wg_zg.at[z_rows],
            wg_zg.at[z_rows],
            z_send.at[n_z - 1 + d - 1],
            z_recv.at[n_z - 1 + d - 1],
            z_peers[d - 1],
        )
        for d in range(1, n_z)
    ]
    for copy in zg_copies:
        copy.start()

    for copy in tabg_copies:
        copy.wait()
    tab_core_copy = send(
        tab_zg, tab_cg, core_send.at[2], core_recv.at[2], core_peer
    )
    tab_core_copy.start()

    mine_s[...] = mm(own_t_ref[...], win_s[...]).astype(BF16)
    for copy in back:
        copy.wait()
    mine_s[...] += mm(gather_t_ref[...], back_s[...]).astype(BF16)

    for copy in zg_copies:
        copy.wait()
    lat_rows = pl.ds(pl.multiple_of(lat * part, 16), part)
    wg_lg[lat_rows] = wg_zg[...]
    latg_copies = [
        send(
            wg_zg,
            wg_lg.at[lat_rows],
            lat_send.at[n_lat - 1 + d - 1],
            lat_recv.at[n_lat - 1 + d - 1],
            lat_peers[d - 1],
        )
        for d in range(1, n_lat)
    ]
    for copy in latg_copies:
        copy.start()

    def finish(w, carry):
        rows = pl.ds(pl.multiple_of(w * WTOK, 16), WTOK)
        values = x_ref[rows, :model_width].astype(F32)
        out_ref[rows] = (values + mine_s[rows, :model_width].astype(F32)).astype(BF16)
        shifted = values - jnp.mean(values, -1, keepdims=True)
        inv_std = lax.rsqrt(jnp.mean(shifted * shifted, -1, keepdims=True) + 1e-05)
        normed = shifted * inv_std
        scaled = mine_s[rows, model_width:].astype(F32) * gain_ref[...]
        glat_ref[rows] = (
            x_ref[rows, model_width:].astype(F32)
            + inv_std
            * (
                scaled
                - jnp.mean(scaled, -1, keepdims=True)
                - normed * jnp.mean(scaled * normed, -1, keepdims=True)
            )
        ).astype(BF16)
        return carry

    lax.fori_loop(0, windows, finish, 0)

    tab_core_copy.wait()
    tab_s[tab_mine] = tab_zg[...]
    tab_s[tab_other] = tab_cg[...]
    gtab_ref[...] = tab_s[...]
    last = tab_s[0:16].astype(F32)
    ggain_ref[...] = jnp.concatenate(
        [last[CELL : CELL + 1], last[CELL + 1 : CELL + 2, : model_width - tab_width]], 1
    )

    for copy in latg_copies:
        copy.wait()
    wg_core_copy = send(
        wg_lg, wg_cg, core_send.at[3], core_recv.at[3], core_peer
    )
    wg_core_copy.start()
    wg_core_copy.wait()
    wg_s[wg_mine] = wg_lg[...]
    wg_s[wg_other] = wg_cg[...]
    for member in range(3):
        gqkv_ref[member] = wg_s[member * model_width : (member + 1) * model_width].astype(F32)
    for p in range(out_parts):
        first = 3 * model_width + p * local_width
        gout_ref[:, p * local_width : (p + 1) * local_width] = wg_s[
            first : first + local_width
        ].astype(F32)


def fused(joined, ln_gain, w_qkv, w_out, table, region, layout):
    gather, own, arrived, starts = layout
    tokens, both = joined.shape
    model_width = both // 2
    local_width = w_out.shape[0]
    heads = local_width // HD
    windows = tokens // WTOK
    n_lon, n_lat, n_tp = (lax.axis_size(name) for name in ("lon", "lat", "tp"))
    n_z = n_lon // 2
    halo_rows = gather.shape[0]
    weight_rows = 3 * model_width + (model_width // local_width) * local_width
    half = weight_rows // 2
    part = half // n_lat
    piece = part // n_z
    tab_rows = windows * heads * 16
    tab_width = round_up(WIDE, 128)
    tab_half = tab_rows // 2
    cfg = (heads, windows, starts, n_lon, n_lat, n_tp)
    vmem = pl.BlockSpec(memory_space=pltpu.VMEM)
    dma = pltpu.SemaphoreType.DMA
    constants = [
        jnp.asarray(m, BF16)
        for m in (gather, own, arrived, gather.T.copy(), own.T.copy(), arrived.T.copy())
    ]
    return pl.pallas_call(
        lambda *refs: fused_kernel(cfg, *refs),
        in_specs=[vmem] * 13,
        out_specs=[vmem] * 6,
        out_shape=[
            jax.ShapeDtypeStruct((tokens, model_width), BF16),
            jax.ShapeDtypeStruct((tokens, model_width), BF16),
            jax.ShapeDtypeStruct((3, model_width, local_width), F32),
            jax.ShapeDtypeStruct((local_width, model_width), F32),
            jax.ShapeDtypeStruct((tab_rows, tab_width), BF16),
            jax.ShapeDtypeStruct((1, model_width), F32),
        ],
        scratch_shapes=[
            pltpu.VMEM((halo_rows, both), BF16),
            pltpu.VMEM((halo_rows, both), BF16),
            pltpu.VMEM((halo_rows, both), BF16),
            pltpu.VMEM((tokens, both), BF16),
            pltpu.VMEM((tokens, model_width), BF16),
            pltpu.VMEM((3, tokens, local_width), BF16),
            pltpu.VMEM((tokens, local_width), BF16),
            pltpu.VMEM((heads, WTOK, WTOK), F32),
            pltpu.VMEM((heads, 16, tab_width), F32),
            pltpu.VMEM((tokens, both), BF16),
            pltpu.VMEM((tokens, both), BF16),
            pltpu.VMEM((weight_rows, local_width), BF16),
            pltpu.VMEM((half, local_width), BF16),
            pltpu.VMEM((half, local_width), BF16),
            pltpu.VMEM((n_lat - 1, part, local_width), BF16),
            pltpu.VMEM((part, local_width), BF16),
            pltpu.VMEM((n_z - 1, piece, local_width), BF16),
            pltpu.VMEM((part, local_width), BF16),
            pltpu.VMEM((half, local_width), BF16),
            pltpu.VMEM((half, local_width), BF16),
            pltpu.VMEM((tab_rows, tab_width), BF16),
            pltpu.VMEM((tab_half, tab_width), BF16),
            pltpu.VMEM((tab_half, tab_width), BF16),
            pltpu.VMEM((n_z - 1, tab_half // n_z, tab_width), BF16),
            pltpu.VMEM((tab_half, tab_width), BF16),
            pltpu.VMEM((tab_half, tab_width), BF16),
            pltpu.VMEM((n_lat * n_tp, 8, model_width), F32),
            dma((3,)),
            dma((3,)),
            dma((windows,)),
            dma((windows,)),
            dma((3,)),
            dma((3,)),
            dma((4,)),
            dma((4,)),
            dma((2 * (n_lat - 1),)),
            dma((2 * (n_lat - 1),)),
            dma((2 * (n_z - 1),)),
            dma((2 * (n_z - 1),)),
            dma((2 * (n_z - 1),)),
            dma((2 * (n_z - 1),)),
            dma((n_lat * n_tp - 1,)),
            dma((n_lat * n_tp - 1,)),
        ],
        compiler_params=pltpu.CompilerParams(
            vmem_limit_bytes=48 * 1024 * 1024, collective_id=0, has_side_effects=True
        ),
        cost_estimate=pl.CostEstimate(
            flops=8 * 10**9, bytes_accessed=16 * 10**6, transcendentals=331776
        ),
    )(
        joined,
        ln_gain.reshape(1, -1),
        w_qkv,
        w_out,
        table,
        region[:, :, None],
        region[:, None, :],
        *constants,
    )


def on_device(latent, cotangent, ln_gain, w_qkv, w_out, bias_table):
    lon_cells, lat_cells, lev_cells, model_width = latent.shape
    head_count = w_out.shape[0] // HD
    lat_bands = lat_cells // WLAT
    lev_bands = lev_cells // WLEV
    lon_bands = lon_cells // WLON
    windows = lat_bands * lev_bands * lon_bands
    spread = spread_matrices()
    layout = halo_layout(lon_cells, lat_cells, lev_cells)
    joined = jnp.concatenate(
        [latent.reshape(-1, model_width), cotangent.reshape(-1, model_width)], 1
    )

    last_device = lax.axis_index("lat") == lax.axis_size("lat") - 1
    position = np.arange(WTOK)
    lat_edge = position % WLAT >= WLAT - WLAT // 2
    lev_edge = position // WLAT % WLEV >= WLEV - WLEV // 2
    lat_last = last_device & (jnp.arange(lat_bands) == lat_bands - 1)
    lev_last = jnp.arange(lev_bands) == lev_bands - 1
    region = (
        2.0 * (lat_last[:, None] & lat_edge).astype(F32)[:, None]
        + (lev_last[:, None] & lev_edge).astype(F32)[None]
    )
    region = jnp.broadcast_to(region[:, :, None], (lat_bands, lev_bands, lon_bands, WTOK))
    region = region.reshape(windows, WTOK)

    grouped = bias_table.reshape(
        lat_bands, lev_bands, head_count, WLEV, WLEV, WLAT, WLAT * NDIFF
    )
    table = sum(
        jnp.einsum(
            "abhtrd,dw->abhtrw", grouped[:, :, :, :, lev], spread[lev], precision=lax.Precision.HIGHEST
        )
        for lev in range(WLEV)
    )
    table = table.reshape(lat_bands * lev_bands, head_count, CELL, WIDE)
    if lon_bands > 1:
        table = jnp.repeat(table, lon_bands, axis=0)

    output, grad_latent, grad_wqkv, grad_wout, grad_tab, grad_gain = fused(
        joined, ln_gain, w_qkv, w_out, table, region, layout
    )
    grad_tab = grad_tab.reshape(lat_bands * lev_bands, lon_bands, head_count, 16, -1)
    grad_tab = grad_tab[:, :, :, :CELL, :WIDE]
    if lon_bands > 1:
        grad_tab = jnp.sum(grad_tab.astype(F32), 1).astype(BF16)
    grad_tab = grad_tab.reshape(lat_bands, lev_bands, head_count, WLEV, WLAT, WIDE)
    grad_bias = jnp.stack(
        [
            jnp.einsum(
                "abhtrw,dw->abhtrd", grad_tab, spread[lev].astype(BF16), preferred_element_type=F32
            )
            for lev in range(WLEV)
        ],
        axis=4,
    ).reshape(bias_table.shape)
    return (
        output.reshape(latent.shape),
        grad_latent.reshape(latent.shape),
        grad_gain.reshape(ln_gain.shape),
        grad_wqkv,
        grad_wout,
        grad_bias,
    )


def solution(mesh):
    return jax.shard_map(
        on_device,
        mesh=mesh,
        in_specs=(
            P("lon", "lat", None, None),
            P("lon", "lat", None, None),
            P(),
            P(None, None, "tp"),
            P("tp", None),
            P("lat", None, "tp", None),
        ),
        out_specs=(
            P("lon", "lat", None, None),
            P("lon", "lat", None, None),
            P(),
            P(None, None, "tp"),
            P("tp", None),
            P("lat", None, "tp", None),
        ),
        check_vma=False,
    )
```

time: 293 us -> 103 us (0.35)
  waiting for transfers between devices: 190 us -> 0 us
  Pallas kernels: 13.7 us -> 85.3 us
  blocking collectives: 31.3 us -> 0 us
  between operations: 14.3 us -> 0.86 us
  other arithmetic: 14.2 us -> 2.79 us
  starting transfers between devices: 8.12 us -> 0 us
  local copies, waits for them, and re-layouts: 18.4 us -> 11.3 us
    psum x3 -> x0, waiting for transfers between devices: 186 us -> none  [the longest x1 91.3 us: on_device(): lax.psum((grad_qkv_local, grad_out_local), ('lon', 'lat'))]
    pallas_call x1, Pallas kernels: 13.7 us -> 85.3 us  [fused(): pl.pallas_call(lambda *refs: fused_kernel(cfg, *refs), in_specs=[vmem] *...]
    psum x1 -> x0, blocking collectives: 31.3 us -> none  [on_device(): grad_gain = lax.psum(gain_local, ('lon', 'lat'))]
    ppermute x6 -> x0, starting transfers between devices: 8 us -> none  [shift_along(): return lax.ppermute(shard, ('lon', 'lat'), pairs)]
    convert_element_type x3 -> x0, other arithmetic: 5.37 us -> none  [the longest x1 2.45 us: on_device(): grad_wqkv.astype(F32)]
    reshape x11 -> x4, local copies, waits for them, and re-layouts: 6.51 us -> 2.18 us  [the longest x1 0.95 us: on_device(): output.reshape(latent.shape)]
    ppermute x6 -> x0, waiting for transfers between devices: 4.12 us -> none  [shift_along(): return lax.ppermute(shard, ('lon', 'lat'), pairs)]
    slice x5 -> x0, local copies, waits for them, and re-layouts: 3.71 us -> none  [the longest x1 2.06 us: leave(): values = jnp.roll(values, WLEV // 2, axis=2)]
  transfers between devices with their start and end apart: 9 -> 0, of which waited for: 5 -> 0; matrix products, arithmetic and copies ran while one was open for 5% -> 0% of each run, Pallas kernels for 0% -> 0%
where the time goes in v2:
time: 103 us
  Pallas kernels  85.3 us (83%)
  local copies, waits for them, and re-layouts  11.3 us (11%)
  other arithmetic  2.79 us (3%)
  matrix products  2.6 us (3%)
    pallas_call x1, Pallas kernels, fused(): pl.pallas_call(lambda *refs: fused_kernel(cfg, *refs), in_specs=[vmem] *...  85.3 us
    unnamed x32, local copies, waits for them, and re-layouts  6.24 us
    dot_general x2, matrix products, on_device(): jnp.einsum('abhtrd,dw->abhtrw', grouped[:, :, :, :, lev], spread[lev], pr...  2.13 us

profile of v2, /device:TPU:0, one launch (start us, length us, event | category | flops | bytes accessed | tf_op | source)
XLA Modules:
  0.0 102.8 jit_solution(4944517386286412326)
XLA Ops:
  0.6 0.0 copy-start.13
  0.7 0.8 and_convert_fusion
  1.5 0.7 and_select_fusion
  2.2 0.2 add.43.refs_5_
  2.4 1.4 %reshape.153 = f32[2,2,4,2,2,6,138]{6,5,4,3,2,1,0:T(8,128)S(1)} reshape(f32[2,2,4,3312]{3,2,1,0:T(4,128)} %param.23) | data formatting | bytes 423936 | tf_op jit(solution)/shard_map/reshape | solution.py:636
  3.9 1.5 %fusion.1 = f32[276,2,2,4,2,6]{0,5,4,3,2,1:T(8,128)S(1)} fusion(f32[138,276,1,1,1,1]{1,0,5,4,3,2:T(8,128)} %constant.49, f32[2,2,4,2,2,6,138]{6,5,4,3,2,1,0:T(8,128)S(1)} %reshape.153), kind=kOutput, calls=%fused_computation.8 | convolution fusion | flops 87754752 | bytes 626464 | tf_op jit(solution)/shard_map/abhtrd,dw->abhtrw/dot_general | solution.py:640
  5.4 0.0 copy-done.13
  5.4 0.0 copy-start.9
  5.4 0.6 fusion
  6.0 0.0 copy-start.10
  6.1 0.1 copy.26
  6.2 0.3 copy-done.9
  6.5 0.1 reshape.150
  6.6 0.5 copy-done.10
  7.2 0.0 copy-start
  7.2 0.0 copy-start.1
  7.2 0.0 copy-start.4
  7.2 0.1 reshape.151
  7.3 0.0 copy-start.2
  7.3 0.0 copy-start.3
  7.3 0.0 copy-start.5
  7.3 1.2 %pad_maximum_fusion.refs_0_ = bf16[576,1024]{1,0:T(8,128)(2,1)} fusion(bf16[576,512]{1,0:T(8,128)(2,1)S(1)} %reshape.151, bf16[576,512]{1,0:T(8,128)(2,1)S(1)} %reshape.150), kind=kLoop, calls=%fused_computation.2 | loop fusion | flops 2359296 | bytes 2359296 | tf_op jit(solution)/shard_map/concatenate | solution.py:619
  8.5 0.0 copy-done
  8.5 0.0 copy-done.1
  8.5 0.0 copy-done.4
  8.5 0.2 copy-done.2
  8.8 0.4 copy-done.3
  9.2 0.1 copy-done.5
  9.3 0.0 copy-start.6
  9.3 1.0 copy-done.6
  10.4 0.0 copy-start.7
  10.4 1.0 copy-done.7
  11.4 85.3 %shard_map.217 = (bf16[576,512]{1,0:T(8,128)(2,1)S(1)}, bf16[576,512]{1,0:T(8,128)(2,1)S(1)}, f32[3,512,256]{2,1,0:T(8,128)}, f32[256,512]{1,0:T(8,128)S(1)}, bf...) custom-call(bf16[576,1024]{1,0:T(8,128)(2,1)} %pad_maximum_fusion.refs_0_, f32[1,512]{1,0:T(1,128)S(1)} %bitcast.40, ...), custom_call_target="tpu_custom_call" | custom-call | flops 8000000000 | bytes 16000000 | tf_op jit(solution)/shard_map/pallas_call | solution.py:535
  96.7 0.0 copy-start.12
  96.7 0.0 copy-start.11
  96.7 1.0 reshape.155
  97.6 0.1 copy.39
  97.7 0.0 copy-done.12
  97.7 0.2 convolution_bitcast_fusion
  98.0 0.0 copy-done.11
  98.0 0.2 convolution_bitcast_fusion.1
  98.2 0.1 pad_maximum_fusion.1
  98.3 0.0 copy-start.8
  98.3 0.1 copy.32
  98.4 1.0 reshape.160
  99.4 1.0 reshape.156
  100.3 0.6 copy.47
  100.9 0.0 copy-done.8
  100.9 1.1 %copy.48 = f32[3,512,256]{2,1,0:T(8,128)} copy(f32[3,512,256]{2,1,0:T(8,128)S(1)} %copy-done.8) | data formatting | bytes 3145728
  102.1 0.8 copy.49
  (5 shorter events, 0.1 us)
Async XLA Ops:
  0.6 4.8 %copy-start.13 = (f32[138,276,1,1,1,1]{1,0,5,4,3,2:T(8,128)S(1)}, f32[138,276,1,1,1,1]{1,0,5,4,3,2:T(8,128)}, u32[]{:S(2)}) copy-start(f32[138,276,1,1,1,1]{1,0,5,4,3,2:T(8,128)} %constant.50) | copy-start | bytes 457060
  5.4 1.1 %copy-start.9 = (bf16[12,12,4,512]{3,2,1,0:T(4,128)(2,1)S(1)}, bf16[12,12,4,512]{3,2,1,0:T(4,128)(2,1)}, u32[]{:S(2)}) copy-start(bf16[12,12,4,512]{3,2,1,0:T(4,128)(2,1)} %param.18) | copy-start | bytes 1769476
  6.0 1.1 %copy-start.10 = (bf16[12,12,4,512]{3,2,1,0:T(4,128)(2,1)S(1)}, bf16[12,12,4,512]{3,2,1,0:T(4,128)(2,1)}, u32[]{:S(2)}) copy-start(bf16[12,12,4,512]{3,2,1,0:T(4,128)(2,1)} %param.19) | copy-start | bytes 1769476
  7.2 1.4 %copy-start = (bf16[256,512]{1,0:T(8,128)(2,1)S(1)}, bf16[256,512]{1,0:T(8,128)(2,1)}, u32[]{:S(2)}) copy-start(bf16[256,512]{1,0:T(8,128)(2,1)} %refs_3_.1) | copy-start | bytes 786436
  7.2 1.4 %copy-start.1 = (f32[512]{0:T(512)S(1)}, f32[512]{0:T(512)}, u32[]{:S(2)}) copy-start(f32[512]{0:T(512)} %param.20) | copy-start | bytes 6148
  7.2 1.4 %copy-start.4 = (bf16[384,576]{1,0:T(8,128)(2,1)S(1)}, bf16[384,576]{1,0:T(8,128)(2,1)}, u32[]{:S(2)}) copy-start(bf16[384,576]{1,0:T(8,128)(2,1)} %constant.44.clone.refs_12_) | copy-start | bytes 1327108
  7.3 1.5 %copy-start.2 = (bf16[576,576]{1,0:T(8,128)(2,1)S(1)}, bf16[576,576]{1,0:T(8,128)(2,1)}, u32[]{:S(2)}) copy-start(bf16[576,576]{1,0:T(8,128)(2,1)} %constant.43.clone.refs_11_) | copy-start | bytes 1990660
  7.3 1.9 %copy-start.3 = (bf16[576,576]{1,0:T(8,128)(2,1)S(1)}, bf16[576,576]{1,0:T(8,128)(2,1)}, u32[]{:S(2)}) copy-start(bf16[576,576]{1,0:T(8,128)(2,1)} %constant.40.clone.refs_8_) | copy-start | bytes 1990660
  7.3 2.0 %copy-start.5 = (bf16[384,576]{1,0:T(8,128)(2,1)S(1)}, bf16[384,576]{1,0:T(8,128)(2,1)}, u32[]{:S(2)}) copy-start(bf16[384,576]{1,0:T(8,128)(2,1)} %constant.39.clone.refs_7_) | copy-start | bytes 1327108
  9.3 1.0 copy-start.6
  10.4 1.0 copy-start.7
  96.7 1.0 %copy-start.12 = (bf16[138,276,1,1,1,1]{1,0,5,4,3,2:T(8,128)(2,1)S(1)}, bf16[138,276,1,1,1,1]{1,0,5,4,3,2:T(8,128)(2,1)}, u32[]{:S(2)}) copy-start(bf16[138,276,1,1,1,1]{1,0,5,4,3,2:T(8,128)(2,1)} %constant.52) | copy-start | bytes 228532
  96.7 1.3 %copy-start.11 = (bf16[138,276,1,1,1,1]{1,0,5,4,3,2:T(8,128)(2,1)S(1)}, bf16[138,276,1,1,1,1]{1,0,5,4,3,2:T(8,128)(2,1)}, u32[]{:S(2)}) copy-start(bf16[138,276,1,1,1,1]{1,0,5,4,3,2:T(8,128)(2,1)} %constant.51) | copy-start | bytes 228532
  98.3 2.6 %copy-start.8 = (f32[3,512,256]{2,1,0:T(8,128)S(1)}, f32[3,512,256]{2,1,0:T(8,128)}, u32[]{:S(2)}) copy-start(f32[3,512,256]{2,1,0:T(8,128)} %get-tuple-element.27) | copy-start | bytes 4718596

commit v3 on v0

v3 whole, which is shorter than its diff:
```python
import math

import jax
import jax.numpy as jnp
import numpy as np
from jax import lax
from jax.experimental import pallas as pl
from jax.experimental.pallas import tpu as pltpu
from jax.sharding import PartitionSpec as P

HD = 64
WLON = 12
WLAT = 6
WLEV = 2
WTOK = 144
NREL = 3312
NDIFF = 2 * WLON - 1
CELL = WLAT * WLEV
WIDE = NDIFF * CELL
F32 = jnp.float32
BF16 = jnp.bfloat16


def spread_matrices():
    spread = np.zeros((WLEV, WLAT * NDIFF, WIDE), np.float32)
    for lev in range(WLEV):
        for row in range(WLAT):
            for diff in range(NDIFF):
                spread[lev, row * NDIFF + diff, diff * CELL + lev * WLAT + row] = 1.0
    return spread


def mm(a, b):
    return lax.dot_general(a, b, (((1,), (0,)), ((), ())), preferred_element_type=F32)


def mm_nt(a, b):
    return lax.dot_general(a, b, (((1,), (1,)), ((), ())), preferred_element_type=F32)


def mm_tn(a, b):
    return lax.dot_general(a, b, (((0,), (0,)), ((), ())), preferred_element_type=F32)


def round_up(count, to):
    return -(-count // to) * to


def halo_layout(lon_cells, lat_cells, lev_cells):
    lon_half, lat_half, lev_half = WLON // 2, WLAT // 2, WLEV // 2
    tokens = lon_cells * lat_cells * lev_cells
    cells = np.arange(tokens).reshape(lon_cells, lat_cells, lev_cells)
    pieces = [
        cells[:lon_half, lat_half:],
        cells[lon_half:, :lat_half],
        cells[:lon_half, :lat_half],
    ]
    starts, total = [], 0
    for piece in pieces:
        starts.append((total, round_up(piece.size, 16)))
        total += round_up(piece.size, 16)
    gather = np.zeros((total, tokens), np.float32)
    slots = []
    for piece, (start, _) in zip(pieces, starts):
        gather[start + np.arange(piece.size), piece.reshape(-1)] = 1.0
        slots.append(tokens + start + np.arange(piece.size).reshape(piece.shape))
    near = np.concatenate([cells[lon_half:, lat_half:], slots[1]], 1)
    far = np.concatenate([slots[0], slots[2]], 1)
    rolled = np.roll(np.concatenate([near, far], 0), -lev_half, axis=2)
    lonb, latb, levb = lon_cells // WLON, lat_cells // WLAT, lev_cells // WLEV
    order = rolled.reshape(lonb, WLON, latb, WLAT, levb, WLEV)
    order = order.transpose(2, 4, 0, 1, 5, 3).reshape(-1)
    place = np.zeros((tokens, tokens + total), np.float32)
    place[np.arange(tokens), order] = 1.0
    return gather, place[:, :tokens], place[:, tokens:], starts


class Refs:
    pass


def fused_kernel(cfg, names, *refs):
    heads, windows, starts, n_lon, n_lat, n_tp, bands = cfg
    lat_bands, lev_bands, lon_bands = bands
    r = Refs()
    for name, ref in zip(names, refs):
        setattr(r, name, ref)
    n_z = n_lon // 2
    model_width = r.gain.shape[1]
    local_width = r.wout.shape[0]
    inv_scale = 1.0 / math.sqrt(HD)
    lon, lat, tp = lax.axis_index("lon"), lax.axis_index("lat"), lax.axis_index("tp")
    z, core = lax.div(lon, 2), lax.rem(lon, 2)
    sibling = lon + 1 - 2 * core
    group = lat * n_tp + tp

    def device(lon_at, lat_at, tp_at):
        return {"lon": lon_at, "lat": lat_at, "tp": tp_at}

    def send(src, dst, sems, index, where):
        return pltpu.make_async_remote_copy(
            src_ref=src,
            dst_ref=dst,
            send_sem=sems.at[0, index],
            recv_sem=sems.at[1, index],
            device_id=where,
            device_id_type=pl.DeviceIdType.MESH,
        )

    def aligned(start, size):
        return pl.ds(pl.multiple_of(start, 16), size)

    lon_next, lon_prev = lax.rem(lon + 1, n_lon), lax.rem(lon + n_lon - 1, n_lon)
    lat_next, lat_prev = lax.rem(lat + 1, n_lat), lax.rem(lat + n_lat - 1, n_lat)
    before = [
        device(lon_prev, lat, tp),
        device(lon, lat_prev, tp),
        device(lon_prev, lat_prev, tp),
    ]
    after = [
        device(lon_next, lat, tp),
        device(lon, lat_next, tp),
        device(lon_next, lat_next, tp),
    ]
    z_peers = [device(lax.rem(z + d, n_z) * 2 + core, lat, tp) for d in range(1, n_z)]
    lat_peers = [device(lon, lax.rem(lat + d, n_lat), tp) for d in range(1, n_lat)]
    group_peers = []
    for d in range(1, n_lat * n_tp):
        other = lax.rem(group + d, n_lat * n_tp)
        group_peers.append(device(lon, lax.div(other, n_tp), lax.rem(other, n_tp)))
    core_peer = device(sibling, lat, tp)
    tp_peer = device(lon, lat, lax.rem(tp + 1, n_tp))

    barrier = pltpu.get_barrier_semaphore()
    greeted = before + after + z_peers + group_peers + [core_peer]
    for where in greeted:
        pl.semaphore_signal(
            barrier, inc=1, device_id=where, device_id_type=pl.DeviceIdType.MESH
        )
    loads = [
        pltpu.make_async_copy(getattr(r, name + "_hbm"), getattr(r, name), r.load_sem.at[i])
        for i, name in enumerate(MATRICES)
    ]
    for copy in loads:
        copy.start()
    loads[0].wait()
    r.pack[...] = mm(r.gather[...], r.x[...]).astype(BF16)
    pl.semaphore_wait(barrier, len(greeted))
    halo = [
        send(r.pack.at[pl.ds(a, n)], r.halo.at[pl.ds(a, n)], r.in_sem, i, before[i])
        for i, (a, n) in enumerate(starts)
    ]
    for copy in halo:
        copy.start()
    wout_copy = send(r.wout, r.wout_their, r.wo_sem, 0, tp_peer)
    wout_copy.start()
    for copy in loads[1:]:
        copy.wait()
    r.win[...] = mm(r.own[...], r.x[...]).astype(BF16)

    types = lat_bands * lev_bands
    run = WLAT * NDIFF
    for kind in range(types):
        block = r.bias_in.at[kind // lev_bands, kind % lev_bands]
        for lev_t in range(WLEV):
            for lev_u in range(WLEV):
                for row in range(WLAT):
                    first = ((lev_t * WLEV + lev_u) * WLAT + row) * run
                    rows = block[:, first : first + run]
                    for head in range(heads):
                        r.table_in[
                            lev_u, kind * heads + head, lev_t * WLAT + row : lev_t * WLAT + row + 1, :
                        ] = rows[head : head + 1]
    total = None
    for lev_u in range(WLEV):
        rest = r.table_in[lev_u].reshape(types * heads * 16, run)
        for _ in range(3):
            piece = rest.astype(BF16)
            rest = rest - piece.astype(F32)
            term = mm(piece, r.spread[lev_u])
            total = term if total is None else total + term
    r.table[...] = total.reshape(types * heads, 16, WIDE)

    for copy in halo:
        copy.wait()
    r.win[...] += mm(r.arrived[...], r.halo[...]).astype(BF16)

    def att_copy(w):
        rows = aligned(w * WTOK, WTOK)
        return send(r.att.at[rows], r.att_their.at[rows], r.att_sem, w, tp_peer)

    def gh_copy(w):
        rows = aligned(w * WTOK, WTOK)
        return send(r.gh.at[rows], r.gh_their.at[rows], r.gh_sem, w, tp_peer)

    def forward(w, carry):
        rows = aligned(w * WTOK, WTOK)
        x = r.win[rows, :model_width].astype(F32)
        cot = r.win[rows, model_width:]
        shifted = x - jnp.mean(x, -1, keepdims=True)
        inv_std = lax.rsqrt(jnp.mean(shifted * shifted, -1, keepdims=True) + 1e-05)
        normed = shifted * inv_std
        r.normed[rows] = normed
        hidden = (normed * r.gain[...]).astype(BF16)
        r.hidden[rows] = hidden
        queries = mm(hidden, r.wqkv[0]).astype(BF16)
        keys = mm(hidden, r.wqkv[1]).astype(BF16)
        vals = mm(hidden, r.wqkv[2]).astype(BF16)
        down = mm_nt(cot, r.wout[...]).astype(BF16)
        r.query[rows] = queries
        r.key[rows] = keys
        kind = lax.div(w, lon_bands)
        last_lat = (lat == n_lat - 1) & (lax.div(kind, lev_bands) == lat_bands - 1)
        last_lev = lax.rem(kind, lev_bands) == lev_bands - 1
        lat_flag = jnp.where(last_lat, 2.0, 0.0)
        lev_flag = jnp.where(last_lev, 1.0, 0.0)
        col = r.col[:, 0:1] * lat_flag + r.col[:, 1:2] * lev_flag
        row = r.row[0:1] * lat_flag + r.row[1:2] * lev_flag
        allowed = col == row
        att_parts, gv_parts = [], []
        for head in range(heads):
            cols = slice(head * HD, (head + 1) * HD)
            q, k, v, d = queries[:, cols], keys[:, cols], vals[:, cols], down[:, cols]
            table = r.table[kind * heads + head]
            for lon_pos in range(WLON):
                start = (WLON - 1 - lon_pos) * CELL
                r.ds[w * heads + head, lon_pos * CELL : (lon_pos + 1) * CELL, :] = table[
                    :CELL, start : start + WTOK
                ]
            scores = mm_nt(q, k) * inv_scale + r.ds[w * heads + head]
            scores = jnp.where(allowed, scores, -jnp.inf)
            expsum = jnp.exp(scores - jnp.max(scores, -1, keepdims=True))
            probs = expsum / jnp.sum(expsum, -1, keepdims=True)
            low = probs.astype(BF16)
            att_parts.append(mm(low, v).astype(BF16))
            dp = mm_nt(d, v)
            gv_parts.append(mm_tn(low, d).astype(BF16))
            r.ds[w * heads + head] = probs * (dp - jnp.sum(dp * probs, -1, keepdims=True))
        r.att[rows] = jnp.concatenate(att_parts, 1)
        att_copy(w).start()
        r.grads[2, rows] = jnp.concatenate(gv_parts, 1)
        return carry

    lax.fori_loop(0, windows, forward, 0)

    blocks = local_width // 128

    class Chunk:
        def __init__(self, index):
            self.base = index * 4
            self.index = index
            rows = r.wg.shape[1]
            self.half, self.part = rows // 2, rows // 2 // n_lat
            self.piece = self.part // n_z
            self.full = r.wg.at[index]
            self.mine = aligned(core * self.half, self.half)
            self.other = aligned((1 - core) * self.half, self.half)
            self.lat_rows = aligned(lat * self.part, self.part)
            self.z_rows = aligned(z * self.piece, self.piece)
            i = index
            self.core_a = send(self.full.at[self.other], r.wg_core.at[i], r.core_sem, 2 * i, core_peer)
            self.core_b = send(r.wg_lg.at[i], r.wg_cg.at[i], r.core_sem, 2 * i + 1, core_peer)
            lat_base, z_base = i * 2 * (n_lat - 1), i * 2 * (n_z - 1)
            self.lat_a, self.lat_b, self.z_a, self.z_b = [], [], [], []
            for d in range(1, n_lat):
                rows_d = aligned(lax.rem(lat + d, n_lat) * self.part, self.part)
                self.lat_a.append(
                    send(r.wg_a.at[i, rows_d], r.wg_lat.at[i, d - 1], r.lat_sem, lat_base + d - 1, lat_peers[d - 1])
                )
                self.lat_b.append(
                    send(
                        r.wg_zg.at[i],
                        r.wg_lg.at[i, self.lat_rows],
                        r.lat_sem,
                        lat_base + n_lat - 1 + d - 1,
                        lat_peers[d - 1],
                    )
                )
            for d in range(1, n_z):
                rows_d = aligned(lax.rem(z + d, n_z) * self.piece, self.piece)
                self.z_a.append(
                    send(r.wg_b.at[i, rows_d], r.wg_z.at[i, d - 1], r.z_sem, z_base + d - 1, z_peers[d - 1])
                )
                self.z_b.append(
                    send(
                        r.wg_zg.at[i, self.z_rows],
                        r.wg_zg.at[i, self.z_rows],
                        r.z_sem,
                        z_base + n_z - 1 + d - 1,
                        z_peers[d - 1],
                    )
                )

        def to_core(self):
            self.core_a.start()

        def to_lat(self):
            self.core_a.wait()
            i = self.index
            r.wg_a[i] = (self.full[self.mine].astype(F32) + r.wg_core[i].astype(F32)).astype(BF16)
            for copy in self.lat_a:
                copy.start()

        def to_z(self):
            for copy in self.lat_a:
                copy.wait()
            i = self.index
            total = r.wg_a[i, self.lat_rows].astype(F32)
            for d in range(1, n_lat):
                total = total + r.wg_lat[i, d - 1].astype(F32)
            r.wg_b[i] = total.astype(BF16)
            for copy in self.z_a:
                copy.start()

        def from_z(self):
            for copy in self.z_a:
                copy.wait()
            i = self.index
            total = r.wg_b[i, self.z_rows].astype(F32)
            for d in range(1, n_z):
                total = total + r.wg_z[i, d - 1].astype(F32)
            r.wg_zg[i, self.z_rows] = total.astype(BF16)
            for copy in self.z_b:
                copy.start()

        def from_lat(self):
            for copy in self.z_b:
                copy.wait()
            r.wg_lg[self.index, self.lat_rows] = r.wg_zg[self.index]
            for copy in self.lat_b:
                copy.start()

        def from_core(self):
            for copy in self.lat_b:
                copy.wait()
            self.core_b.start()

        def end(self):
            self.core_b.wait()
            self.full[self.mine] = r.wg_lg[self.index]
            self.full[self.other] = r.wg_cg[self.index]

    def put(chunk, first, grad):
        size = grad.shape[0]
        for b in range(grad.shape[1] // 128):
            r.wg[chunk, first + b * size : first + (b + 1) * size] = grad[
                :, b * 128 : (b + 1) * 128
            ].astype(BF16)

    def take(chunk, first, ref, size, columns):
        for b in range(columns // 128):
            ref[:, b * 128 : (b + 1) * 128] = r.wg[
                chunk, first + b * size : first + (b + 1) * size
            ].astype(F32)

    one, two = Chunk(0), Chunk(1)
    second = blocks * model_width
    put(0, 0, mm_tn(r.hidden[...], r.grads[2]))
    put(0, second, mm_tn(r.att[...], r.win[:, model_width:]))
    one.to_core()

    r.gain_part[group] = jnp.zeros(r.gain_part.shape[1:], F32)

    def backward(w, carry):
        rows = aligned(w * WTOK, WTOK)
        gq_parts, gk_parts = [], []
        for head in range(heads):
            cols = slice(head * HD, (head + 1) * HD)
            r.gtab[head] = jnp.zeros(r.gtab.shape[1:], F32)
            for lon_pos in range(WLON):
                start = (WLON - 1 - lon_pos) * CELL
                r.gtab[head, :CELL, start : start + WTOK] += r.ds[
                    w * heads + head, lon_pos * CELL : (lon_pos + 1) * CELL, :
                ]
            r.tab[aligned((w * heads + head) * 16, 16)] = r.gtab[head].astype(BF16)
            ds_low = r.ds[w * heads + head].astype(BF16)
            q, k = r.query[rows, cols], r.key[rows, cols]
            gq_parts.append((mm(ds_low, k) * inv_scale).astype(BF16))
            gk_parts.append((mm_tn(ds_low, q) * inv_scale).astype(BF16))
        gq = jnp.concatenate(gq_parts, 1)
        gk = jnp.concatenate(gk_parts, 1)
        r.grads[0, rows] = gq
        r.grads[1, rows] = gk
        gh = mm_nt(gq, r.wqkv[0])
        gh = gh + mm_nt(gk, r.wqkv[1])
        gh = (gh + mm_nt(r.grads[2, rows], r.wqkv[2])).astype(BF16)
        r.gh[rows] = gh
        gh_copy(w).start()
        r.gain_part[group, 0:1] += jnp.sum(gh.astype(F32) * r.normed[rows], 0, keepdims=True)
        return carry

    middle = windows // 2
    lax.fori_loop(0, middle, backward, 0)
    one.to_lat()
    lax.fori_loop(middle, windows, backward, 0)

    gain_copies = [
        send(r.gain_part.at[group], r.gain_part.at[group], r.gain_sem, i, where)
        for i, where in enumerate(group_peers)
    ]
    for copy in gain_copies:
        copy.start()
    put(1, 0, mm_tn(r.hidden[...], r.grads[0]))
    put(1, second, mm_tn(r.hidden[...], r.grads[1]))
    two.to_core()
    one.to_z()

    def arrive_att(w, carry):
        att_copy(w).wait()
        return carry

    wout_copy.wait()
    lax.fori_loop(0, windows, arrive_att, 0)
    mine = mm(r.att[...], r.wout[...]).astype(BF16)
    theirs = mm(r.att_their[...], r.wout_their[...]).astype(BF16)
    r.sums[:, :model_width] = (mine.astype(F32) + theirs.astype(F32)).astype(BF16)
    two.to_lat()

    def leave(index, columns):
        r.back[index] = mm(r.arrived_t[...], r.sums[:, columns]).astype(BF16)
        copies = [
            send(
                r.back.at[index, pl.ds(a, n)],
                r.came.at[index, pl.ds(a, n)],
                r.out_sem,
                3 * index + i,
                after[i],
            )
            for i, (a, n) in enumerate(starts)
        ]
        for copy in copies:
            copy.start()
        return copies

    out_copies = leave(0, slice(0, model_width))

    for copy in gain_copies:
        copy.wait()
    gain_total = r.gain_part[0, 0:1]
    for i in range(1, n_lat * n_tp):
        gain_total = gain_total + r.gain_part[i, 0:1]
    tab_width = r.tab.shape[1]
    spare = jnp.concatenate([gain_total, jnp.zeros((1, 2 * tab_width - model_width), F32)], 1)
    r.gtab[0] = r.tab[0:16].astype(F32)
    r.gtab[0, CELL : CELL + 1] = spare[:, :tab_width]
    r.gtab[0, CELL + 1 : CELL + 2] = spare[:, tab_width:]
    r.tab[0:16] = r.gtab[0].astype(BF16)
    tab_half = r.tab.shape[0] // 2
    tab_piece = tab_half // n_z
    tab_mine = aligned(core * tab_half, tab_half)
    tab_other = aligned((1 - core) * tab_half, tab_half)
    tab_rows = aligned(z * tab_piece, tab_piece)
    tab_a = send(r.tab.at[tab_other], r.tab_core, r.core_sem, 4, core_peer)
    tab_a.start()

    one.from_z()
    two.to_z()
    tab_a.wait()
    r.tab_a[...] = (r.tab[tab_mine].astype(F32) + r.tab_core[...].astype(F32)).astype(BF16)
    tabz = [
        send(
            r.tab_a.at[aligned(lax.rem(z + d, n_z) * tab_piece, tab_piece)],
            r.tab_z.at[d - 1],
            r.tz_sem,
            d - 1,
            z_peers[d - 1],
        )
        for d in range(1, n_z)
    ]
    for copy in tabz:
        copy.start()

    def arrive_gh(w, carry):
        gh_copy(w).wait()
        return carry

    lax.fori_loop(0, windows, arrive_gh, 0)
    r.sums[:, model_width:] = (r.gh[...].astype(F32) + r.gh_their[...].astype(F32)).astype(BF16)
    gh_copies = leave(1, slice(model_width, 2 * model_width))
    r.back_own[...] = mm(r.own_t[...], r.sums[...]).astype(BF16)

    one.from_lat()
    for copy in tabz:
        copy.wait()
    total = r.tab_a[tab_rows].astype(F32)
    for d in range(1, n_z):
        total = total + r.tab_z[d - 1].astype(F32)
    r.tab_zg[tab_rows] = total.astype(BF16)
    tabg = [
        send(
            r.tab_zg.at[tab_rows],
            r.tab_zg.at[tab_rows],
            r.tz_sem,
            n_z - 1 + d - 1,
            z_peers[d - 1],
        )
        for d in range(1, n_z)
    ]
    for copy in tabg:
        copy.start()
    two.from_z()

    for copy in out_copies:
        copy.wait()
    out_own = r.back_own[:, :model_width] + mm(r.gather_t[...], r.came[0]).astype(BF16)
    r.out[...] = (r.x[:, :model_width].astype(F32) + out_own.astype(F32)).astype(BF16)

    one.from_core()
    for copy in tabg:
        copy.wait()
    tab_b = send(r.tab_zg, r.tab_cg, r.core_sem, 5, core_peer)
    tab_b.start()

    for copy in gh_copies:
        copy.wait()
    r.gh_own[...] = r.back_own[:, model_width:] + mm(r.gather_t[...], r.came[1]).astype(BF16)
    two.from_lat()

    def finish(w, carry):
        rows = aligned(w * WTOK, WTOK)
        values = r.x[rows, :model_width].astype(F32)
        shifted = values - jnp.mean(values, -1, keepdims=True)
        inv_std = lax.rsqrt(jnp.mean(shifted * shifted, -1, keepdims=True) + 1e-05)
        normed = shifted * inv_std
        scaled = r.gh_own[rows].astype(F32) * r.gain[...]
        r.glat[rows] = (
            r.x[rows, model_width:].astype(F32)
            + inv_std
            * (
                scaled
                - jnp.mean(scaled, -1, keepdims=True)
                - normed * jnp.mean(scaled * normed, -1, keepdims=True)
            )
        ).astype(BF16)
        return carry

    lax.fori_loop(0, windows, finish, 0)

    one.end()
    take(0, 0, r.gqkv.at[2], model_width, local_width)
    take(0, second, r.gout, local_width, model_width)

    tab_b.wait()
    r.tab[tab_mine] = r.tab_zg[...]
    r.tab[tab_other] = r.tab_cg[...]
    last = r.tab[0:16].astype(F32)
    r.ggain[...] = jnp.concatenate(
        [last[CELL : CELL + 1], last[CELL + 1 : CELL + 2, : model_width - tab_width]], 1
    )
    for lev_u in range(WLEV):
        r.table_out[lev_u] = mm_nt(r.tab[:, :WIDE], r.spread[lev_u]).reshape(
            windows * heads, 16, run
        )
    for kind in range(types):
        block = r.gbias.at[kind // lev_bands, kind % lev_bands]
        for lev_t in range(WLEV):
            for lev_u in range(WLEV):
                for row in range(WLAT):
                    first = ((lev_t * WLEV + lev_u) * WLAT + row) * run
                    cell = lev_t * WLAT + row
                    for head in range(heads):
                        total = None
                        for c in range(lon_bands):
                            at = (kind * lon_bands + c) * heads + head
                            term = r.table_out[lev_u, at, cell : cell + 1, :]
                            total = term if total is None else total + term
                        block[head : head + 1, first : first + run] = total

    two.from_core()
    two.end()
    take(1, 0, r.gqkv.at[0], model_width, local_width)
    take(1, second, r.gqkv.at[1], model_width, local_width)


MATRICES = ("gather", "own", "arrived", "gather_t", "own_t", "arrived_t", "spread")


def fused(joined, ln_gain, w_qkv, w_out, bias_table, layout, bands):
    gather, own, arrived, starts = layout
    tokens, both = joined.shape
    width = both // 2
    local = w_out.shape[0]
    heads = local // HD
    windows = tokens // WTOK
    n_lon, n_lat, n_tp = (lax.axis_size(name) for name in ("lon", "lat", "tp"))
    n_z = n_lon // 2
    types = bands[0] * bands[1]
    run = WLAT * NDIFF
    halo_rows = gather.shape[0]
    chunk = 2 * (local // 128) * width
    half = chunk // 2
    part = half // n_lat
    piece = part // n_z
    tab_rows = windows * heads * 16
    tab_width = round_up(WIDE, 128)
    tab_half = tab_rows // 2
    cfg = (heads, windows, starts, n_lon, n_lat, n_tp, bands)
    position = np.arange(WTOK)
    edges = np.stack(
        [
            position % WLAT >= WLAT - WLAT // 2,
            position // WLAT % WLEV >= WLEV - WLEV // 2,
        ]
    ).astype(np.float32)
    matrices = {
        "gather": gather,
        "own": own,
        "arrived": arrived,
        "gather_t": gather.T.copy(),
        "own_t": own.T.copy(),
        "arrived_t": arrived.T.copy(),
        "spread": spread_matrices(),
    }
    vmem = pl.BlockSpec(memory_space=pltpu.VMEM)
    anywhere = pl.BlockSpec(memory_space=pl.ANY)

    def sems(count):
        return pltpu.SemaphoreType.DMA((2, count))

    operands = {
        "x": joined,
        "gain": ln_gain.reshape(1, -1),
        "wqkv": w_qkv,
        "wout": w_out,
        "bias_in": bias_table,
        "col": jnp.asarray(edges.T.copy()),
        "row": jnp.asarray(edges),
    }
    for name in MATRICES:
        operands[name + "_hbm"] = jnp.asarray(matrices[name], BF16)
    results = {
        "out": ((tokens, width), BF16),
        "glat": ((tokens, width), BF16),
        "ggain": ((1, width), F32),
        "gqkv": ((3, width, local), F32),
        "gout": ((local, width), F32),
        "gbias": (bias_table.shape, F32),
    }
    scratch = {name: pltpu.VMEM(matrices[name].shape, BF16) for name in MATRICES}
    for name, shape, dtype in (
        ("pack", (halo_rows, both), BF16),
        ("halo", (halo_rows, both), BF16),
        ("back", (2, halo_rows, width), BF16),
        ("came", (2, halo_rows, width), BF16),
        ("win", (tokens, both), BF16),
        ("sums", (tokens, both), BF16),
        ("back_own", (tokens, both), BF16),
        ("gh_own", (tokens, width), BF16),
        ("normed", (tokens, width), F32),
        ("hidden", (tokens, width), BF16),
        ("query", (tokens, local), BF16),
        ("key", (tokens, local), BF16),
        ("grads", (3, tokens, local), BF16),
        ("att", (tokens, local), BF16),
        ("att_their", (tokens, local), BF16),
        ("wout_their", (local, width), BF16),
        ("gh", (tokens, width), BF16),
        ("gh_their", (tokens, width), BF16),
        ("ds", (windows * heads, WTOK, WTOK), F32),
        ("gtab", (heads, 16, tab_width), F32),
        ("table_in", (WLEV, types * heads, 16, run), F32),
        ("table", (types * heads, 16, WIDE), F32),
        ("table_out", (WLEV, windows * heads, 16, run), F32),
        ("wg", (2, chunk, 128), BF16),
        ("wg_core", (2, half, 128), BF16),
        ("wg_a", (2, half, 128), BF16),
        ("wg_lat", (2, n_lat - 1, part, 128), BF16),
        ("wg_b", (2, part, 128), BF16),
        ("wg_z", (2, n_z - 1, piece, 128), BF16),
        ("wg_zg", (2, part, 128), BF16),
        ("wg_lg", (2, half, 128), BF16),
        ("wg_cg", (2, half, 128), BF16),
        ("tab", (tab_rows, tab_width), BF16),
        ("tab_core", (tab_half, tab_width), BF16),
        ("tab_a", (tab_half, tab_width), BF16),
        ("tab_z", (n_z - 1, tab_half // n_z, tab_width), BF16),
        ("tab_zg", (tab_half, tab_width), BF16),
        ("tab_cg", (tab_half, tab_width), BF16),
        ("gain_part", (n_lat * n_tp, 8, width), F32),
    ):
        scratch[name] = pltpu.VMEM(shape, dtype)
    for name, count in (
        ("in_sem", 3),
        ("wo_sem", 1),
        ("att_sem", windows),
        ("gh_sem", windows),
        ("out_sem", 6),
        ("core_sem", 6),
        ("lat_sem", 4 * (n_lat - 1)),
        ("z_sem", 4 * (n_z - 1)),
        ("tz_sem", 2 * (n_z - 1)),
        ("gain_sem", n_lat * n_tp - 1),
    ):
        scratch[name] = sems(count)
    scratch["load_sem"] = pltpu.SemaphoreType.DMA((len(MATRICES),))
    names = list(operands) + list(results) + list(scratch)
    return pl.pallas_call(
        lambda *refs: fused_kernel(cfg, names, *refs),
        in_specs=[anywhere if name.endswith("_hbm") else vmem for name in operands],
        out_specs=[vmem] * len(results),
        out_shape=[jax.ShapeDtypeStruct(*spec) for spec in results.values()],
        scratch_shapes=list(scratch.values()),
        compiler_params=pltpu.CompilerParams(
            vmem_limit_bytes=56 * 1024 * 1024, collective_id=0, has_side_effects=True
        ),
        cost_estimate=pl.CostEstimate(
            flops=8 * 10**9, bytes_accessed=16 * 10**6, transcendentals=331776
        ),
    )(*operands.values())


def on_device(latent, cotangent, ln_gain, w_qkv, w_out, bias_table):
    lon_cells, lat_cells, lev_cells, model_width = latent.shape
    bands = (lat_cells // WLAT, lev_cells // WLEV, lon_cells // WLON)
    layout = halo_layout(lon_cells, lat_cells, lev_cells)
    joined = jnp.concatenate(
        [latent.reshape(-1, model_width), cotangent.reshape(-1, model_width)], 1
    )
    output, grad_latent, grad_gain, grad_wqkv, grad_wout, grad_bias = fused(
        joined, ln_gain, w_qkv, w_out, bias_table, layout, bands
    )
    return (
        output.reshape(latent.shape),
        grad_latent.reshape(latent.shape),
        grad_gain.reshape(ln_gain.shape),
        grad_wqkv,
        grad_wout,
        grad_bias,
    )


def solution(mesh):
    return jax.shard_map(
        on_device,
        mesh=mesh,
        in_specs=(
            P("lon", "lat", None, None),
            P("lon", "lat", None, None),
            P(),
            P(None, None, "tp"),
            P("tp", None),
            P("lat", None, "tp", None),
        ),
        out_specs=(
            P("lon", "lat", None, None),
            P("lon", "lat", None, None),
            P(),
            P(None, None, "tp"),
            P("tp", None),
            P("lat", None, "tp", None),
        ),
        check_vma=False,
    )
```

time: 551 us -> 80.4 us (0.15)
  the two profiles are of different devices: /device:TPU:0 before, /device:TPU:27 now
where the time goes in v3:
time: 80.4 us; the launch traced here: 80.2 us
  Pallas kernels  68.6 us (85%)
  local copies, waits for them, and re-layouts  9.7 us (12%)
  other arithmetic  1.19 us (1%)
    pallas_call x1, Pallas kernels, fused(): pl.pallas_call(lambda *refs: fused_kernel(cfg, names, *refs), in_specs=[a...  68.6 us
    unnamed x14, local copies, waits for them, and re-layouts  3.44 us
    reshape x1, local copies, waits for them, and re-layouts, on_device(): output.reshape(latent.shape)  2.37 us
    reshape x1, local copies, waits for them, and re-layouts, on_device(): grad_latent.reshape(latent.shape)  2.24 us

profile of v3, /device:TPU:27, one launch (start us, length us, event | category | flops | bytes accessed | tf_op | source)
XLA Modules:
  0.0 80.2 jit_solution(17904998517520465744)
XLA Ops:
  0.6 0.0 copy-start.1
  0.6 1.5 %reshape.30 = bf16[576,512]{1,0:T(8,128)(2,1)S(1)} reshape(bf16[12,12,4,512]{3,2,1,0:T(4,128)(2,1)} %param.15) | data formatting | bytes 1179648 | tf_op jit(solution)/shard_map/reshape | solution.py:717
  2.2 0.0 copy-done.1
  2.2 0.1 reshape.31
  2.3 1.2 %pad_maximum_fusion.refs_0_ = bf16[576,1024]{1,0:T(8,128)(2,1)} fusion(bf16[576,512]{1,0:T(8,128)(2,1)S(1)} %reshape.31, bf16[576,512]{1,0:T(8,128)(2,1)S(1)} %reshape.30), kind=kLoop, calls=%fused_computation | loop fusion | flops 2359296 | bytes 2359296 | tf_op jit(solution)/shard_map/concatenate | solution.py:716
  3.5 68.6 %shard_map.190 = (bf16[576,512]{1,0:T(8,128)(2,1)}, bf16[576,512]{1,0:T(8,128)(2,1)}, f32[1,512]{1,0:T(1,128)}, f32[3,512,256]{2,1,0:T(8,128)}, f32[256,512]{1,0:T(8,128)}, /*index=5*/f32[2,2,4,3312]{3,2,1,0:T(4,128)}) custom-call(bf16[576,1024]{1,0:T(8,128)(2,1)} %pad_maximum_fusion.refs_0_, f32[1,512]{1,0:T(1,128)} %bitcast.3, ...), custom_call_target="tpu_custom_call" | custom-call | flops 8000000000 | bytes 16000000 | tf_op jit(solution)/shard_map/pallas_call | solution.py:697
  72.1 0.0 copy-start.4
  72.1 0.0 copy-start
  72.1 2.4 %reshape.33 = bf16[12,12,4,512]{3,2,1,0:T(4,128)(2,1)} reshape(bf16[576,512]{1,0:T(8,128)(2,1)} %get-tuple-element.12) | data formatting | bytes 1179648 | tf_op jit(solution)/shard_map/reshape | solution.py:723
  74.5 2.2 %reshape.34 = bf16[12,12,4,512]{3,2,1,0:T(4,128)(2,1)} reshape(bf16[576,512]{1,0:T(8,128)(2,1)} %get-tuple-element.13) | data formatting | bytes 1179648 | tf_op jit(solution)/shard_map/reshape | solution.py:724
  76.7 0.0 copy-done.4
  76.7 0.6 copy.25
  77.3 0.0 copy-done
  77.3 0.0 copy-start.2
  77.3 0.0 copy-start.3
  77.3 1.1 %copy.26 = f32[3,512,256]{2,1,0:T(8,128)} copy(f32[3,512,256]{2,1,0:T(8,128)S(1)} %copy-done) | data formatting | bytes 3145728
  78.5 0.2 copy-done.2
  78.7 0.8 copy.27
  79.5 0.0 copy-done.3
  79.5 0.7 copy.28
Async XLA Ops:
  0.6 1.5 %copy-start.1 = (bf16[12,12,4,512]{3,2,1,0:T(4,128)(2,1)S(1)}, bf16[12,12,4,512]{3,2,1,0:T(4,128)(2,1)}, u32[]{:S(2)}) copy-start(bf16[12,12,4,512]{3,2,1,0:T(4,128)(2,1)} %param.16) | copy-start | bytes 1769476
  72.1 4.6 %copy-start.4 = (f32[1,512]{1,0:T(1,128)S(1)}, f32[1,512]{1,0:T(1,128)}, u32[]{:S(2)}) copy-start(f32[1,512]{1,0:T(1,128)} %get-tuple-element.14) | copy-start | bytes 6148
  72.1 5.2 %copy-start = (f32[3,512,256]{2,1,0:T(8,128)S(1)}, f32[3,512,256]{2,1,0:T(8,128)}, u32[]{:S(2)}) copy-start(f32[3,512,256]{2,1,0:T(8,128)} %get-tuple-element.27) | copy-start | bytes 4718596
  77.3 1.4 %copy-start.2 = (f32[256,512]{1,0:T(8,128)S(1)}, f32[256,512]{1,0:T(8,128)}, u32[]{:S(2)}) copy-start(f32[256,512]{1,0:T(8,128)} %get-tuple-element.28) | copy-start | bytes 1572868
  77.3 2.2 %copy-start.3 = (f32[2,2,4,3312]{3,2,1,0:T(4,128)S(1)}, f32[2,2,4,3312]{3,2,1,0:T(4,128)}, u32[]{:S(2)}) copy-start(f32[2,2,4,3312]{3,2,1,0:T(4,128)} %get-tuple-element.29) | copy-start | bytes 635908
